TPU v7x, 32 devices: a whole 2x2x4 slice. The times are simulated.
32 devices in a mesh: tile: 8 (over z, y), head: 4 (over x, core).
Axes of the slice: x: 2, y: 2, z: 4, core: 2. Of those that a mesh axis runs over, the one named last changes fastest.
Arguments:
- query_slab: bfloat16 [32, 2, 32, 5120], P('tile', None, 'head'), may hold values from -30 to 30
- key_slab: bfloat16 [32, 2, 32, 5120], P('tile', None, 'head'), may hold values from -5 to 5
- value_slab: bfloat16 [32, 2, 32, 5120], P('tile', None, 'head'), may hold values from -5 to 5
- upstream: bfloat16 [2048, 5120], P('tile', 'head'), may hold values from -5 to 5
Outputs:
- attended: bfloat16 [2048, 5120], P('tile', 'head')
- query_grad: bfloat16 [2048, 5120], P('tile', 'head')
- key_grad: bfloat16 [2048, 5120], P('tile', 'head')
- value_grad: bfloat16 [2048, 5120], P('tile', 'head')
All inputs are finite; a program needn't handle non-finite values.
Results may differ from a plain program's by a relative error of at most 0.012.
Values may be sent and summed in bfloat16 or wider, within the bound.
A program may use at most 128 MiB of HBM per device.

v0:
```python
import jax
import jax.numpy as jnp
from jax import lax
from jax.sharding import PartitionSpec as P

HEAD_DIM = 128
FRAMES = 8
FRAME_W = 32


masked_score = -1e30


def from_behind(value, axis, steps):
    count = lax.axis_size(axis)
    leading, last = (max(0, -steps), min(count, count - steps))
    return lax.ppermute(value, axis, [(source, source + steps) for source in range(leading, last)])


def to_tiles(grid, tile_rows, tile_cols):
    features = grid.shape[-1]
    shaped = grid.reshape(FRAMES, tile_rows, 4, tile_cols, 4, features)
    return shaped.transpose(1, 3, 0, 2, 4, 5).reshape(tile_rows, tile_cols, FRAMES * 16, features)


def from_tiles(tiles):
    tile_rows = tiles.shape[0]
    tile_cols = tiles.shape[1]
    features = tiles.shape[-1]
    shaped = tiles.reshape(tile_rows, tile_cols, FRAMES, 4, 4, features)
    return shaped.transpose(2, 0, 3, 1, 4, 5).reshape(FRAMES * tile_rows * tile_cols * 16, features)


def window_keys(nearby, tile_rows, tile_cols):
    features = nearby.shape[-1]
    shaped = nearby.reshape(2, FRAMES, tile_rows + 2, 4, tile_cols + 2, 4, features)
    pieces = [
        shaped[:, :, row_step : row_step + tile_rows, :, col_step : col_step + tile_cols]
        for row_step in range(3)
        for col_step in range(3)
    ]
    stacked = jnp.stack(pieces, axis=1)
    ordered = stacked.transpose(0, 3, 5, 1, 2, 4, 6, 7)
    return ordered.reshape(2, tile_rows, tile_cols, 144 * FRAMES, features)


def fold_keys(window, tile_rows, tile_cols):
    features = window.shape[-1]
    portions = window.reshape(tile_rows, tile_cols, 3, 3, FRAMES, 4, 4, features)
    accumulated = jnp.zeros((FRAMES, tile_rows + 2, 4, tile_cols + 2, 4, features), jnp.float32)
    for row_step in range(3):
        for col_step in range(3):
            portion = portions[:, :, row_step, col_step].transpose(2, 0, 3, 1, 4, 5)
            accumulated = accumulated.at[
                :, row_step : row_step + tile_rows, :, col_step : col_step + tile_cols
            ].add(portion)
    return accumulated.reshape(FRAMES, 4 * (tile_rows + 2), 4 * (tile_cols + 2), features)


def key_mask(tile_rows, tile_cols, row_first, col_first, rows_all, cols_all):
    row_index = jnp.arange(tile_rows, dtype=jnp.int32)[:, None, None, None]
    col_index = jnp.arange(tile_cols, dtype=jnp.int32)[None, :, None, None]
    row_steps = jnp.arange(3, dtype=jnp.int32)[None, None, :, None]
    col_steps = jnp.arange(3, dtype=jnp.int32)[None, None, None, :]
    row_place = row_first + row_index + row_steps - 1
    col_place = col_first + col_index + col_steps - 1
    usable = (row_place >= 0) & (row_place < rows_all) & (col_place >= 0) & (col_place < cols_all)
    spread = jnp.broadcast_to(usable[..., None], (tile_rows, tile_cols, 3, 3, FRAMES * 16))
    return spread.reshape(tile_rows, tile_cols, 144 * FRAMES)


def attend(query_blocks, key_window, value_window, grad_blocks, usable):
    tile_rows, pair_count, query_count, features = query_blocks.shape
    head_count = features // HEAD_DIM
    key_count = key_window.shape[2]
    query_heads = query_blocks.reshape(tile_rows, pair_count, query_count, head_count, HEAD_DIM)
    grad_heads = grad_blocks.reshape(tile_rows, pair_count, query_count, head_count, HEAD_DIM)
    key_heads = key_window.reshape(tile_rows, pair_count, key_count, head_count, HEAD_DIM)
    value_heads = value_window.reshape(tile_rows, pair_count, key_count, head_count, HEAD_DIM)
    scaling = HEAD_DIM ** (-0.5)
    scores = (
        jnp.einsum("rcqhd,rckhd->rchqk", query_heads, key_heads, preferred_element_type=jnp.float32)
        * scaling
    )
    scores = jnp.where(usable[:, :, None, None, :], scores, masked_score)
    highest = jnp.max(scores, axis=-1, keepdims=True)
    raised = jnp.exp(scores - highest)
    weights = raised / jnp.sum(raised, axis=-1, keepdims=True)
    weights_low = weights.astype(jnp.bfloat16)
    mixed = jnp.einsum(
        "rchqk,rckhd->rcqhd", weights_low, value_heads, preferred_element_type=jnp.float32
    )
    offsets = jnp.sum(grad_heads.astype(jnp.float32) * mixed, axis=-1).transpose(0, 1, 3, 2)
    weight_grad = jnp.einsum(
        "rcqhd,rckhd->rchqk", grad_heads, value_heads, preferred_element_type=jnp.float32
    )
    score_grad = weights * (weight_grad - offsets[..., None])
    score_low = score_grad.astype(jnp.bfloat16)
    query_grad = (
        jnp.einsum("rchqk,rckhd->rcqhd", score_low, key_heads, preferred_element_type=jnp.float32)
        * scaling
    )
    key_terms = (
        jnp.einsum("rchqk,rcqhd->rckhd", score_low, query_heads, preferred_element_type=jnp.float32)
        * scaling
    )
    value_terms = jnp.einsum(
        "rchqk,rcqhd->rckhd", weights_low, grad_heads, preferred_element_type=jnp.float32
    )
    return (
        mixed.reshape(tile_rows, pair_count, query_count, features),
        query_grad.reshape(tile_rows, pair_count, query_count, features),
        key_terms.reshape(tile_rows, pair_count, key_count, features),
        value_terms.reshape(tile_rows, pair_count, key_count, features),
    )


def pass_keys(block, step):
    return from_behind(block, "tile", step)


def pass_terms(block, step):
    return from_behind(block, "tile", step)


def settle(received):
    rows_here = received.shape[-3]
    width_here = received.shape[-2]
    features = received.shape[-1]
    shaped = received.reshape(FRAMES, 4, rows_here, width_here, features).transpose(0, 2, 1, 3, 4)
    return shaped.reshape(FRAMES, 4 * rows_here, width_here, features)


def local(query_slab, key_slab, value_slab, upstream):
    query_rows, key_rows, value_rows = (
        lax.all_to_all(query_slab, "head", split_axis=3, concat_axis=2, tiled=True),
        lax.all_to_all(key_slab, "head", split_axis=3, concat_axis=2, tiled=True),
        lax.all_to_all(value_slab, "head", split_axis=3, concat_axis=2, tiled=True),
    )
    owner_count = lax.axis_size("tile")
    row_groups = owner_count // 4
    source_count = query_rows.shape[0]
    features = query_rows.shape[3]
    tile_rows = query_rows.shape[1] // row_groups
    tile_cols = FRAME_W // 16
    band_width = 4 * tile_cols
    line_count = 4 * tile_rows
    owner_index = lax.axis_index("tile")
    row_group = owner_index // 4
    col_group = owner_index % 4
    left_ok = col_group > 0
    right_ok = col_group < 3

    def to_owners(slab):
        shaped = slab.reshape(source_count, row_groups, tile_rows, 4, band_width, features)
        return shaped.transpose(1, 3, 0, 2, 4, 5).reshape(
            owner_count, source_count, tile_rows, band_width, features
        )

    query_got, key_got, value_got = (
        lax.all_to_all(to_owners(query_rows), "tile", split_axis=0, concat_axis=1, tiled=True),
        lax.all_to_all(to_owners(key_rows), "tile", split_axis=0, concat_axis=1, tiled=True),
        lax.all_to_all(to_owners(value_rows), "tile", split_axis=0, concat_axis=1, tiled=True),
    )
    owned_query = settle(query_got)
    owned_pair = jnp.stack((settle(key_got), settle(value_got)))
    from_left = pass_keys(owned_pair[:, :, :, band_width - 4 :], 1)
    from_right = pass_keys(owned_pair[:, :, :, 0:4], -1)
    from_left = jnp.where(left_ok, from_left, jnp.zeros_like(from_left))
    from_right = jnp.where(right_ok, from_right, jnp.zeros_like(from_right))
    wide_pair = jnp.concatenate((from_left, owned_pair, from_right), axis=3)
    from_above = pass_keys(wide_pair, 4)
    from_below = pass_keys(wide_pair, -4)
    nearby = jnp.concatenate((from_above, wide_pair, from_below), axis=2)
    query_tiles = to_tiles(owned_query, tile_rows, tile_cols)
    grad_tiles = to_tiles(
        upstream.reshape(FRAMES, line_count, band_width, features), tile_rows, tile_cols
    )
    usable = key_mask(
        tile_rows,
        tile_cols,
        row_group * tile_rows,
        col_group * tile_cols,
        row_groups * tile_rows,
        4 * tile_cols,
    )
    totals = jnp.zeros((2, FRAMES, line_count + 8, band_width + 8, features), jnp.float32)

    def one_column(totals, column):
        first_col = column * 4
        nearby_part = lax.dynamic_slice_in_dim(nearby, first_col, 12, 3)
        windows = window_keys(nearby_part, tile_rows, 1)
        query_part = lax.dynamic_slice_in_dim(query_tiles, column, 1, 1)
        grad_part = lax.dynamic_slice_in_dim(grad_tiles, column, 1, 1)
        usable_part = lax.dynamic_slice_in_dim(usable, column, 1, 1)
        mixed, query_grad, key_terms, value_terms = attend(
            query_part, windows[0], windows[1], grad_part, usable_part
        )
        folded = jnp.stack(
            (fold_keys(key_terms, tile_rows, 1), fold_keys(value_terms, tile_rows, 1))
        )
        current = lax.dynamic_slice_in_dim(totals, first_col, 12, 3)
        totals = lax.dynamic_update_slice_in_dim(totals, current + folded, first_col, 3)
        return (totals, (mixed[:, 0].astype(jnp.bfloat16), query_grad[:, 0].astype(jnp.bfloat16)))

    extended, (mixed, query_grad) = lax.scan(
        one_column, totals, jnp.arange(tile_cols, dtype=jnp.int32)
    )
    attended = from_tiles(jnp.swapaxes(mixed, 0, 1))
    query_out = from_tiles(jnp.swapaxes(query_grad, 0, 1))
    top_band = extended[:, :, 0:4].astype(jnp.bfloat16)
    bottom_band = extended[:, :, line_count + 4 :].astype(jnp.bfloat16)
    terms_below = pass_terms(top_band, -4).astype(jnp.float32)
    terms_above = pass_terms(bottom_band, 4).astype(jnp.float32)
    incoming = terms_above
    incoming = incoming + terms_below
    rowed = extended[:, :, 4 : line_count + 4] + incoming
    left_terms = rowed[:, :, :, 0:4].astype(jnp.bfloat16)
    right_terms = rowed[:, :, :, band_width + 4 :].astype(jnp.bfloat16)
    terms_right = pass_terms(left_terms, -1)
    terms_left = pass_terms(right_terms, 1)
    terms_right = jnp.where(right_ok, terms_right, jnp.zeros_like(terms_right)).astype(jnp.float32)
    terms_left = jnp.where(left_ok, terms_left, jnp.zeros_like(terms_left)).astype(jnp.float32)
    summed = rowed[:, :, :, 4 : band_width + 4]
    summed = summed + jnp.pad(terms_left, ((0, 0), (0, 0), (0, 0), (0, band_width - 4), (0, 0)))
    summed = summed + jnp.pad(terms_right, ((0, 0), (0, 0), (0, 0), (band_width - 4, 0), (0, 0)))
    summed = summed.astype(jnp.bfloat16)
    key_grad = summed[0].reshape(-1, features)
    value_grad = summed[1].reshape(-1, features)
    return (attended, query_out, key_grad, value_grad)


def solution(mesh):
    placed = (
        P("tile", None, "head", None),
        P("tile", None, "head", None),
        P("tile", None, "head", None),
        P("tile", "head"),
    )
    return jax.shard_map(
        local,
        mesh=mesh,
        in_specs=placed,
        out_specs=(P("tile", "head"), P("tile", "head"), P("tile", "head"), P("tile", "head")),
        check_vma=False,
    )
```

profile of v0, /device:TPU:0, one launch (start us, length us, event | category | flops | bytes accessed | tf_op | source)
XLA Modules:
  0.0 836.2 jit_solution(9608438441804621013)
XLA Ops:
  0.6 11.9 %copy.161 = bf16[4,2,8,5120]{2,0,1,3:T(4,128)(2,1)} copy(bf16[4,2,8,5120]{3,2,1,0:T(8,128)(2,1)} %param.43) | data formatting | bytes 1310720 | tf_op args[1]
  12.5 13.8 %reshape.1389 = bf16[4,2,40960]{2,1,0:T(2,128)(2,1)} reshape(bf16[5120,2,4,8]{3,2,1,0:T(4,128)(2,1)} %bitcast.380) | data formatting | bytes 1310720
  30.6 9.9 %copy.163 = bf16[4,2,8,5120]{2,0,1,3:T(4,128)(2,1)} copy(bf16[4,2,8,5120]{3,2,1,0:T(8,128)(2,1)S(1)} %copy-done.10) | data formatting | bytes 1310720 | tf_op args[2]
  40.5 13.8 %reshape.1387 = bf16[4,2,40960]{2,1,0:T(2,128)(2,1)} reshape(bf16[5120,2,4,8]{3,2,1,0:T(4,128)(2,1)} %bitcast.381) | data formatting | bytes 1310720
  57.8 13.7 %reshape.1390 = bf16[5120,2,4,8]{3,2,1,0:T(4,128)(2,1)} reshape(bf16[4,2,40960]{2,1,0:T(2,128)(2,1)S(1)} %all-to-all-done.2) | data formatting | bytes 1310720
  71.5 12.6 %copy.162 = bf16[2,4,4,1,8,1280]{5,4,2,1,0,3:T(8,128)(2,1)} copy(bf16[2,4,4,1,8,1280]{4,2,0,5,1,3:T(4,128)(2,1)} %bitcast.377) | data formatting | bytes 1310720 | tf_op jit(solution)/shard_map/transpose | solution.py:156
  90.7 13.7 %reshape.1388 = bf16[5120,2,4,8]{3,2,1,0:T(4,128)(2,1)} reshape(bf16[4,2,40960]{2,1,0:T(2,128)(2,1)S(1)} %all-to-all-done.4) | data formatting | bytes 1310720
  104.4 11.6 %copy.164 = bf16[2,4,4,1,8,1280]{5,4,2,1,0,3:T(8,128)(2,1)S(1)} copy(bf16[2,4,4,1,8,1280]{4,2,0,5,1,3:T(4,128)(2,1)} %bitcast.378) | data formatting | bytes 1310720 | tf_op jit(solution)/shard_map/transpose | solution.py:156
  116.0 24.0 %all_to_all.72 = bf16[8,4,1,8,1280]{4,3,1,2,0:T(8,128)(2,1)S(1)} all-to-all(bf16[8,4,1,8,1280]{4,3,1,2,0:T(8,128)(2,1)S(1)} %bitcast.398), channel_id=1, replica_groups=mesh['tile'=8,'head'=4] {'tile'}, dimensions={0} | all-to-all | bytes 1310720 | tf_op jit(solution)/shard_map/all_to_all | solution.py:163
  145.7 25.1 %collective-permute-done = bf16[2,8,4,4,1280]{4,3,2,1,0:T(4,128)(2,1)} collective-permute-done((bf16[2,8,4,4,1280]{4,3,2,1,0:T(4,128)(2,1)S(1)}, bf16[2,8,4,4,1280]{4,3,2,1,0:T(4,128)(2,1)}, u32[]{:S(2)}, u32[]{:S(2)}) %collective-permute-start) | collective-permute-done | bytes 655392 | tf_op jit(solution)/shard_map/ppermute | solution.py:17
  177.2 8.5 %collective-permute-start.2 = (bf16[2,8,4,16,1280]{4,3,2,1,0:T(8,128)(2,1)}, bf16[2,8,4,16,1280]{4,3,2,1,0:T(8,128)(2,1)}, u32[]{:S(2)}, u32[]{:S(2)}) collective-permute-start(bf16[2,8,4,16,1280]{4,3,2,1,0:T(8,128)(2,1)} %pad_maximum_fusion.1), channel_id=1, source_target_pairs={{0,16},{4,20},{8,24},{12,28},{1,17},{5,21},{9,25},{13,29},{2,18},{... | collective-permute-start | bytes 7864328 | tf_op jit(solution)/shard_map/ppermute | solution.py:17
  185.6 11.9 %copy.157 = bf16[4,2,8,5120]{2,0,1,3:T(4,128)(2,1)} copy(bf16[4,2,8,5120]{3,2,1,0:T(8,128)(2,1)} %param.42) | data formatting | bytes 1310720 | tf_op args[0]
  197.6 13.1 %reshape.1385 = bf16[4,2,40960]{2,1,0:T(2,128)(2,1)S(1)} reshape(bf16[5120,2,4,8]{3,2,1,0:T(4,128)(2,1)} %bitcast.382) | data formatting | bytes 1310720
  210.7 12.8 %all_to_all.73 = bf16[4,2,40960]{2,1,0:T(2,128)(2,1)S(1)} all-to-all(bf16[4,2,40960]{2,1,0:T(2,128)(2,1)S(1)} %reshape.1385), channel_id=1, replica_groups=mesh['tile'=8,'head'=4] {'head'}, dimensions={0} | all-to-all | bytes 1310720 | tf_op jit(solution)/shard_map/all_to_all | solution.py:136
  223.5 13.6 %reshape.1386 = bf16[5120,2,4,8]{3,2,1,0:T(4,128)(2,1)} reshape(bf16[4,2,40960]{2,1,0:T(2,128)(2,1)S(1)} %all_to_all.73) | data formatting | bytes 1310720
  237.1 12.7 %copy.158 = bf16[2,4,4,1,8,1280]{5,4,2,1,0,3:T(8,128)(2,1)} copy(bf16[2,4,4,1,8,1280]{4,2,0,5,1,3:T(4,128)(2,1)} %bitcast.379) | data formatting | bytes 1310720 | tf_op jit(solution)/shard_map/transpose | solution.py:156
  259.9 48.0 %all-to-all-done.1 = bf16[8,4,1,8,1280]{4,3,1,2,0:T(8,128)(2,1)S(1)} async-done(((bf16[8,4,1,8,1280]{4,3,1,2,0:T(8,128)(2,1)}), bf16[8,4,1,8,1280]{4,3,1,2,0:T(8,128)(2,1)S(1)}, u32[]{:S(2)}, u32[]{:S(2)}) %all-to-all-start.1) | async-done | bytes 655392 | tf_op jit(solution)/shard_map/all_to_all | solution.py:161
  315.1 7.4 copy.167
  329.8 325.1 %while.35 = (s32[]{:T(128)}, f32[2,8,12,16,1280]{4,1,3,2,0:T(8,128)}, bf16[2,1,128,1280]{2,3,1,0:T(8,128)(2,1)}, bf16[2,1,128,1280]{2,3,1,0:T(8,128)(2,1)}, s32[...) while((s32[]{:T(128)}, ...), condition=%wide.region_6.7_spmd, body=%wide.region_0.6_spmd.sunk | while | flops 2291302400 | bytes 457144032 | solution.py:206
  417.5 9.6 %copy.200 = f32[1,1,1152,10,128]{4,3,2,1,0:T(8,128)} copy(f32[1,1,1152,10,128]{2,4,3,1,0:T(8,128)} %convolution_bitcast_fusion.3) | data formatting | bytes 11796480 | tf_op jit(solution)/shard_map/while/body/eval_jaxpr/rchqk,rcqhd->rckhd/transpose | solution.py:107
  427.1 9.3 %reshape.1398 = f32[1,1,3,3,8,4,4,1280]{7,6,5,4,3,2,1,0:T(4,128)} reshape(f32[1,1,1152,10,128]{4,3,2,1,0:T(8,128)} %copy.200) | data formatting | bytes 11796480 | tf_op jit(solution)/shard_map/while/body/eval_jaxpr/reshape;while/body/eval_jaxpr/reshape | solution.py:49
  437.6 9.6 %copy.199 = f32[1,1,1152,10,128]{4,3,2,1,0:T(8,128)} copy(f32[1,1,1152,10,128]{2,4,3,1,0:T(8,128)} %multiply_bitcast_fusion.2) | data formatting | bytes 11796480 | tf_op jit(solution)/shard_map/while/body/eval_jaxpr/mul | solution.py:104
  447.2 9.3 %reshape.1397 = f32[1,1,3,3,8,4,4,1280]{7,6,5,4,3,2,1,0:T(4,128)} reshape(f32[1,1,1152,10,128]{4,3,2,1,0:T(8,128)} %copy.199) | data formatting | bytes 11796480 | tf_op jit(solution)/shard_map/while/body/eval_jaxpr/reshape;while/body/eval_jaxpr/reshape | solution.py:49
  566.1 9.6 %copy.200 = f32[1,1,1152,10,128]{4,3,2,1,0:T(8,128)} copy(f32[1,1,1152,10,128]{2,4,3,1,0:T(8,128)} %convolution_bitcast_fusion.3) | data formatting | bytes 11796480 | tf_op jit(solution)/shard_map/while/body/eval_jaxpr/rchqk,rcqhd->rckhd/transpose | solution.py:107
  575.7 9.3 %reshape.1398 = f32[1,1,3,3,8,4,4,1280]{7,6,5,4,3,2,1,0:T(4,128)} reshape(f32[1,1,1152,10,128]{4,3,2,1,0:T(8,128)} %copy.200) | data formatting | bytes 11796480 | tf_op jit(solution)/shard_map/while/body/eval_jaxpr/reshape;while/body/eval_jaxpr/reshape | solution.py:49
  586.2 9.6 %copy.199 = f32[1,1,1152,10,128]{4,3,2,1,0:T(8,128)} copy(f32[1,1,1152,10,128]{2,4,3,1,0:T(8,128)} %multiply_bitcast_fusion.2) | data formatting | bytes 11796480 | tf_op jit(solution)/shard_map/while/body/eval_jaxpr/mul | solution.py:104
  595.9 9.3 %reshape.1397 = f32[1,1,3,3,8,4,4,1280]{7,6,5,4,3,2,1,0:T(4,128)} reshape(f32[1,1,1152,10,128]{4,3,2,1,0:T(8,128)} %copy.199) | data formatting | bytes 11796480 | tf_op jit(solution)/shard_map/while/body/eval_jaxpr/reshape;while/body/eval_jaxpr/reshape | solution.py:49
  654.9 12.9 %copy.186 = bf16[2,8,12,16,1280]{4,3,2,1,0:T(8,128)(2,1)} copy(f32[2,8,12,16,1280]{4,1,3,2,0:T(8,128)} %get-tuple-element.387) | data formatting | bytes 23592960 | tf_op jit(solution)/shard_map/while | solution.py:206
  681.0 15.6 %copy.173 = f32[2,8,12,16,1280]{4,3,2,1,0:T(8,128)} copy(f32[2,8,12,16,1280]{4,1,3,2,0:T(8,128)} %get-tuple-element.387) | data formatting | bytes 31457280 | tf_op jit(solution)/shard_map/while | solution.py:206
  696.6 37.7 %collective-permute-done.4 = bf16[2,8,4,16,1280]{4,3,2,1,0:T(8,128)(2,1)S(1)} collective-permute-done((bf16[2,8,4,16,1280]{4,3,2,1,0:T(8,128)(2,1)}, bf16[2,8,4,16,1280]{4,3,2,1,0:T(8,128)(2,1)S(1)}, u32[]{:S(2)}, u32[]{:S(2)}) %collective-permute-start.4) | collective-permute-done | bytes 2621472 | tf_op jit(solution)/shard_map/ppermute | solution.py:17
  734.3 61.3 %collective-permute-done.5 = bf16[2,8,4,16,1280]{4,3,2,1,0:T(8,128)(2,1)} collective-permute-done((bf16[2,8,4,16,1280]{4,3,2,1,0:T(8,128)(2,1)}, bf16[2,8,4,16,1280]{4,3,2,1,0:T(8,128)(2,1)}, u32[]{:S(2)}, u32[]{:S(2)}) %collective-permute-start.5) | collective-permute-done | bytes 2621472 | tf_op jit(solution)/shard_map/ppermute | solution.py:17
  812.9 16.9 %collective-permute-done.6 = bf16[2,8,4,4,1280]{4,3,2,1,0:T(4,128)(2,1)} collective-permute-done((bf16[2,8,4,4,1280]{4,3,2,1,0:T(4,128)(2,1)S(1)}, bf16[2,8,4,4,1280]{4,3,2,1,0:T(4,128)(2,1)}, u32[]{:S(2)}, u32[]{:S(2)}) %collective-permute-start.6) | collective-permute-done | bytes 655392 | tf_op jit(solution)/shard_map/ppermute | solution.py:17
  (246 shorter events, 302.7 us)
Async XLA Ops:
  12.5 18.1 %copy-start.10 = (bf16[4,2,8,5120]{3,2,1,0:T(8,128)(2,1)S(1)}, bf16[4,2,8,5120]{3,2,1,0:T(8,128)(2,1)}, u32[]{:S(2)}) copy-start(bf16[4,2,8,5120]{3,2,1,0:T(8,128)(2,1)} %param.44) | copy-start | bytes 1966084
  26.3 27.9 %all-to-all-start.2 = ((bf16[4,2,40960]{2,1,0:T(2,128)(2,1)}), bf16[4,2,40960]{2,1,0:T(2,128)(2,1)S(1)}, u32[]{:S(2)}, u32[]{:S(2)}) async-start(bf16[4,2,40960]{2,1,0:T(2,128)(2,1)} %reshape.1389), calls=%async_computation.2 | async-start | bytes 1310720 | tf_op jit(solution)/shard_map/all_to_all | solution.py:137
  54.3 29.8 %all-to-all-start.4 = ((bf16[4,2,40960]{2,1,0:T(2,128)(2,1)}), bf16[4,2,40960]{2,1,0:T(2,128)(2,1)S(1)}, u32[]{:S(2)}, u32[]{:S(2)}) async-start(bf16[4,2,40960]{2,1,0:T(2,128)(2,1)} %reshape.1387), calls=%async_computation.4 | async-start | bytes 1310720 | tf_op jit(solution)/shard_map/all_to_all | solution.py:138
  84.1 31.9 %all-to-all-start.3 = ((bf16[8,4,1,8,1280]{4,3,1,2,0:T(8,128)(2,1)}), bf16[8,4,1,8,1280]{4,3,1,2,0:T(8,128)(2,1)S(1)}, u32[]{:S(2)}, u32[]{:S(2)}) async-start(bf16[8,4,1,8,1280]{4,3,1,2,0:T(8,128)(2,1)} %bitcast.64), calls=%async_computation.3 | async-start | bytes 1310720 | tf_op jit(solution)/shard_map/all_to_all | solution.py:162
  140.5 30.2 %collective-permute-start = (bf16[2,8,4,4,1280]{4,3,2,1,0:T(4,128)(2,1)S(1)}, bf16[2,8,4,4,1280]{4,3,2,1,0:T(4,128)(2,1)}, u32[]{:S(2)}, u32[]{:S(2)}) collective-permute-start(bf16[2,8,4,4,1280]{4,3,2,1,0:T(4,128)(2,1)S(1)} %get-tuple-element.464), channel_id=1, source_target_pairs={{0,4},{4,8},{8,12},{12,16},{16,20},{20,24},{24,28},{1,5},{5,9},{9,... | collective-permute-start | bytes 1966088 | tf_op jit(solution)/shard_map/ppermute | solution.py:17
  144.3 26.7 %collective-permute-start.1 = (bf16[2,8,4,4,1280]{4,3,2,1,0:T(4,128)(2,1)S(1)}, bf16[2,8,4,4,1280]{4,3,2,1,0:T(4,128)(2,1)}, u32[]{:S(2)}, u32[]{:S(2)}) collective-permute-start(bf16[2,8,4,4,1280]{4,3,2,1,0:T(4,128)(2,1)S(1)} %get-tuple-element.465), channel_id=1, source_target_pairs={{4,0},{8,4},{12,8},{16,12},{20,16},{24,20},{28,24},{5,1},{9,5},{13... | collective-permute-start | bytes 1966088 | tf_op jit(solution)/shard_map/ppermute | solution.py:17
  175.9 134.9 %collective-permute-start.3 = (bf16[2,8,4,16,1280]{4,3,2,1,0:T(8,128)(2,1)}, bf16[2,8,4,16,1280]{4,3,2,1,0:T(8,128)(2,1)}, u32[]{:S(2)}, u32[]{:S(2)}) collective-permute-start(bf16[2,8,4,16,1280]{4,3,2,1,0:T(8,128)(2,1)} %pad_maximum_fusion.1), channel_id=1, source_target_pairs={{16,0},{20,4},{24,8},{28,12},{17,1},{21,5},{25,9},{29,13},{18,2},{... | collective-permute-start | bytes 7864328 | tf_op jit(solution)/shard_map/ppermute | solution.py:17
  177.2 133.6 %collective-permute-start.2 = (bf16[2,8,4,16,1280]{4,3,2,1,0:T(8,128)(2,1)}, bf16[2,8,4,16,1280]{4,3,2,1,0:T(8,128)(2,1)}, u32[]{:S(2)}, u32[]{:S(2)}) collective-permute-start(bf16[2,8,4,16,1280]{4,3,2,1,0:T(8,128)(2,1)} %pad_maximum_fusion.1), channel_id=1, source_target_pairs={{0,16},{4,20},{8,24},{12,28},{1,17},{5,21},{9,25},{13,29},{2,18},{... | collective-permute-start | bytes 7864328 | tf_op jit(solution)/shard_map/ppermute | solution.py:17
  237.1 18.2 %copy-start.4 = (bf16[256,1280]{1,0:T(8,128)(2,1)S(1)}, bf16[256,1280]{1,0:T(8,128)(2,1)}, u32[]{:S(2)}) copy-start(bf16[256,1280]{1,0:T(8,128)(2,1)} %param.45) | copy-start | bytes 1966084
  249.8 58.1 %all-to-all-start.1 = ((bf16[8,4,1,8,1280]{4,3,1,2,0:T(8,128)(2,1)}), bf16[8,4,1,8,1280]{4,3,1,2,0:T(8,128)(2,1)S(1)}, u32[]{:S(2)}, u32[]{:S(2)}) async-start(bf16[8,4,1,8,1280]{4,3,1,2,0:T(8,128)(2,1)} %bitcast.56), calls=%async_computation.1 | async-start | bytes 1310720 | tf_op jit(solution)/shard_map/all_to_all | solution.py:161
  322.6 7.2 copy-start.11
  402.1 4.2 copy-start.1
  402.1 5.3 slice-start.6
  402.1 5.3 slice-start.7
  470.0 17.6 %slice-start = ((s8[15728640]{0:T(1024)(128)(4,1)}), s8[4194304]{0:T(1024)(128)(4,1)S(1)}, s32[]{:S(2)}) async-start(s8[15728640]{0:T(1024)(128)(4,1)} %bitcast.357), calls=%async_computation.6 | async-start | bytes 8388608 | tf_op jit(solution)/shard_map/while
  470.0 17.5 %slice-start.1 = ((s8[15728640]{0:T(1024)(128)(4,1)}), s8[3145728]{0:T(1024)(128)(4,1)S(1)}, s32[]{:S(2)}) async-start(s8[15728640]{0:T(1024)(128)(4,1)} %bitcast.357), calls=%async_computation.7 | async-start | bytes 6291456 | tf_op jit(solution)/shard_map/while
  477.4 10.2 %slice-start.2 = ((s8[15728640]{0:T(1024)(128)(4,1)}), s8[4194304]{0:T(1024)(128)(4,1)S(1)}, s32[]{:S(2)}) async-start(s8[15728640]{0:T(1024)(128)(4,1)} %bitcast.357), calls=%async_computation.8 | async-start | bytes 8388608 | tf_op jit(solution)/shard_map/while
  481.5 6.1 slice-start.3
  492.4 5.4 copy-start
  550.7 4.2 copy-start.1
  550.7 5.3 slice-start.6
  550.7 5.3 slice-start.7
  618.6 17.6 %slice-start = ((s8[15728640]{0:T(1024)(128)(4,1)}), s8[4194304]{0:T(1024)(128)(4,1)S(1)}, s32[]{:S(2)}) async-start(s8[15728640]{0:T(1024)(128)(4,1)} %bitcast.357), calls=%async_computation.6 | async-start | bytes 8388608 | tf_op jit(solution)/shard_map/while
  618.6 17.5 %slice-start.1 = ((s8[15728640]{0:T(1024)(128)(4,1)}), s8[3145728]{0:T(1024)(128)(4,1)S(1)}, s32[]{:S(2)}) async-start(s8[15728640]{0:T(1024)(128)(4,1)} %bitcast.357), calls=%async_computation.7 | async-start | bytes 6291456 | tf_op jit(solution)/shard_map/while
  626.0 10.2 %slice-start.2 = ((s8[15728640]{0:T(1024)(128)(4,1)}), s8[4194304]{0:T(1024)(128)(4,1)S(1)}, s32[]{:S(2)}) async-start(s8[15728640]{0:T(1024)(128)(4,1)} %bitcast.357), calls=%async_computation.8 | async-start | bytes 8388608 | tf_op jit(solution)/shard_map/while
  630.1 6.1 slice-start.3
  641.0 5.4 copy-start
  673.2 61.1 %collective-permute-start.4 = (bf16[2,8,4,16,1280]{4,3,2,1,0:T(8,128)(2,1)}, bf16[2,8,4,16,1280]{4,3,2,1,0:T(8,128)(2,1)S(1)}, u32[]{:S(2)}, u32[]{:S(2)}) collective-permute-start(bf16[2,8,4,16,1280]{4,3,2,1,0:T(8,128)(2,1)} %get-tuple-element.458), channel_id=1, source_target_pairs={{0,16},{4,20},{8,24},{12,28},{1,17},{5,21},{9,25},{13,29},{2,18},{... | collective-permute-start | bytes 7864328 | tf_op jit(solution)/shard_map/ppermute | solution.py:17
  679.7 115.9 %collective-permute-start.5 = (bf16[2,8,4,16,1280]{4,3,2,1,0:T(8,128)(2,1)}, bf16[2,8,4,16,1280]{4,3,2,1,0:T(8,128)(2,1)}, u32[]{:S(2)}, u32[]{:S(2)}) collective-permute-start(bf16[2,8,4,16,1280]{4,3,2,1,0:T(8,128)(2,1)} %get-tuple-element.459), channel_id=1, source_target_pairs={{16,0},{20,4},{24,8},{28,12},{17,1},{21,5},{25,9},{29,13},{18,2},{... | collective-permute-start | bytes 7864328 | tf_op jit(solution)/shard_map/ppermute | solution.py:17
  696.6 110.4 %copy-start.7 = (bf16[2,1,128,1280]{2,3,1,0:T(8,128)(2,1)S(1)}, bf16[2,1,128,1280]{2,3,1,0:T(8,128)(2,1)}, u32[]{:S(2)}) copy-start(bf16[2,1,128,1280]{2,3,1,0:T(8,128)(2,1)} %get-tuple-element.386) | copy-start | bytes 1966084
  803.0 26.8 %collective-permute-start.6 = (bf16[2,8,4,4,1280]{4,3,2,1,0:T(4,128)(2,1)S(1)}, bf16[2,8,4,4,1280]{4,3,2,1,0:T(4,128)(2,1)}, u32[]{:S(2)}, u32[]{:S(2)}) collective-permute-start(bf16[2,8,4,4,1280]{4,3,2,1,0:T(4,128)(2,1)S(1)} %get-tuple-element.460), channel_id=1, source_target_pairs={{0,4},{4,8},{8,12},{12,16},{16,20},{20,24},{24,28},{1,5},{5,9},{9,... | collective-permute-start | bytes 1966088 | tf_op jit(solution)/shard_map/ppermute | solution.py:17
  805.5 24.6 %collective-permute-start.7 = (bf16[2,8,4,4,1280]{4,3,2,1,0:T(4,128)(2,1)S(1)}, bf16[2,8,4,4,1280]{4,3,2,1,0:T(4,128)(2,1)}, u32[]{:S(2)}, u32[]{:S(2)}) collective-permute-start(bf16[2,8,4,4,1280]{4,3,2,1,0:T(4,128)(2,1)S(1)} %get-tuple-element.461), channel_id=1, source_target_pairs={{4,0},{8,4},{12,8},{16,12},{20,16},{24,20},{28,24},{5,1},{9,5},{13... | collective-permute-start | bytes 1966088 | tf_op jit(solution)/shard_map/ppermute | solution.py:17
  (15 other events, 36.0 us)
where the time goes:
time: 853 us; the launch traced here: 836 us
  local copies, waits for them, and re-layouts  421 us (49%)
  waiting for transfers between devices  189 us (22%)
  other arithmetic  75.1 us (9%)
  starting transfers between devices  46.1 us (5%)
  blocking collectives  36.8 us (4%)
  loops' own time  33.9 us (4%)
  matrix products  33 us (4%)
    ppermute x8, waiting for transfers between devices, from_behind(): lax.ppermute(value, axis, [(source, source + steps) for source in range(l...  141 us
    unnamed x19, local copies, waits for them, and re-layouts  116 us
    another operation x20, local copies, waits for them, and re-layouts  61.7 us
    all_to_all x1, waiting for transfers between devices, local(): lax.all_to_all(to_owners(query_rows), 'tile', split_axis=0, concat_axis=1...  48 us
    while x7, local copies, waits for them, and re-layouts, local(): lax.scan(one_column, totals, jnp.arange(tile_cols, dtype=jnp.int32))  43.1 us
    reshape x4, local copies, waits for them, and re-layouts, fold_keys(): window.reshape(tile_rows, tile_cols, 3, 3, FRAMES, 4, 4, features)  37.3 us
    transpose x3, local copies, waits for them, and re-layouts, to_owners(): shaped.transpose(1, 3, 0, 2, 4, 5)  36.9 us
    scatter-add x30, other arithmetic, fold_keys(): accumulated = accumulated.at[:, row_step:row_step + tile_rows, :, col_ste...  34.6 us
  transfers between devices with their start and end apart: 12, of which 5 were waited for; matrix products, arithmetic and copies ran while one was open for 19% of the time, Pallas kernels for 0%

commit v1 on v0

--- a/solution.py
+++ b/solution.py
@@ -1,11 +1,16 @@
+import math
+
 import jax
 import jax.numpy as jnp
 from jax import lax
+from jax.experimental import pallas as pl
+from jax.experimental.pallas import tpu as pltpu
 from jax.sharding import PartitionSpec as P
 
 HEAD_DIM = 128
 FRAMES = 8
 FRAME_W = 32
+MESH = pl.DeviceIdType.MESH
 
 
 masked_score = -1e30
@@ -230,6 +235,384 @@
     return (attended, query_out, key_grad, value_grad)
 
 
+SLOTS = 14
+
+
+def fast_kernel(send_ref, up_ref, out_ref, qkv, gbuf, obuf, acc, landed, rims,
+                main_send, main_recv, ext_send, ext_recv, left_send, left_recv, right_send, right_recv,
+                up_send, up_recv, upx_send, upx_recv, out_send, out_recv, outx_send, outx_recv,
+                rim_send, rim_recv):
+    tile = lax.axis_index("tile")
+    head = lax.axis_index("head")
+    me = tile * 4 + head
+    row_half = tile // 4
+    col = tile % 4
+
+    barrier = pltpu.get_barrier_semaphore()
+
+    def greet(step, carry):
+        other = (me + step) % 32
+        pl.semaphore_signal(barrier, inc=1, device_id=(other // 4, other % 4), device_id_type=MESH)
+        return carry
+
+    lax.fori_loop(1, 32, greet, 0)
+    pl.semaphore_wait(barrier, 31)
+
+    def push(src, dst, send_sem, recv_sem, to_tile, to_head):
+        return pltpu.make_async_remote_copy(
+            src_ref=src, dst_ref=dst, send_sem=send_sem, recv_sem=recv_sem,
+            device_id=(to_tile, to_head), device_id_type=MESH)
+
+    def landing(dst, recv_sem):
+        return pltpu.make_async_copy(dst, dst, recv_sem)
+
+    def main_copy(other):
+        to_tile, to_head = other // 4, other % 4
+        src = send_ref.at[to_head * 10 + to_tile]
+        dst = qkv.at[:, pl.ds(1 + 2 * head, 2), tile]
+        return push(src, dst, main_send.at[other], main_recv.at[me], to_tile, to_head)
+
+    def main_start(step, carry):
+        main_copy((me + step) % 32).start()
+        return carry
+
+    lax.fori_loop(1, 32, main_start, 0)
+    pltpu.make_async_copy(send_ref.at[head * 10 + tile], qkv.at[:, pl.ds(1 + 2 * head, 2), tile],
+                          main_recv.at[me]).start()
+
+    rows = pl.ds(16 * row_half, 16)
+
+    def up_copy(other):
+        return push(up_ref.at[other], gbuf.at[pl.ds(1 + 2 * col, 2), :, rows],
+                    up_send.at[other], up_recv.at[tile], other, head)
+
+    def up_start(step, carry):
+        up_copy((tile + step) % 8).start()
+        return carry
+
+    lax.fori_loop(1, 8, up_start, 0)
+    pltpu.make_async_copy(up_ref.at[tile], gbuf.at[pl.ds(1 + 2 * col, 2), :, rows], up_recv.at[tile]).start()
+
+    def upx_copy(extra):
+        return push(up_ref.at[8 + extra], gbuf.at[pl.ds(11, 2), :, rows],
+                    upx_send.at[extra], upx_recv.at[row_half], 4 * extra + col, head)
+
+    for extra in range(2):
+        @pl.when(row_half == extra)
+        def _(extra=extra):
+            pltpu.make_async_copy(up_ref.at[8 + extra], gbuf.at[pl.ds(11, 2), :, rows],
+                                  upx_recv.at[row_half]).start()
+
+        @pl.when(row_half != extra)
+        def _(extra=extra):
+            upx_copy(extra).start()
+
+    def ext_parts(which):
+        to_head, extra = which // 2, which % 2
+        return to_head, extra, to_head * 10 + 8 + extra
+
+    def ext_copy(which):
+        to_head, extra, source = ext_parts(which)
+        return push(send_ref.at[source], qkv.at[:, pl.ds(11, 2), tile],
+                    ext_send.at[which], ext_recv.at[tile], 4 * extra + head, to_head)
+
+    def ext_is_own(which):
+        to_head, extra, source = ext_parts(which)
+        return (4 * extra + head) * 4 + to_head == me
+
+    def left_copy(which):
+        to_head, extra, source = ext_parts(which)
+        return push(send_ref.at[source, pl.ds(1, 2), 1], qkv.at[pl.ds(1, 2), 10, tile],
+                    left_send.at[which], left_recv.at[tile], 4 * extra + head + 1, to_head)
+
+    def left_is_own(which):
+        to_head, extra, source = ext_parts(which)
+        return (4 * extra + head + 1) * 4 + to_head == me
+
+    def right_copy(which):
+        to_head, extra, source = ext_parts(which)
+        return push(send_ref.at[source, pl.ds(1, 2), 0], qkv.at[pl.ds(1, 2), 13, tile],
+                    right_send.at[which], right_recv.at[tile], 4 * extra + head - 1, to_head)
+
+    def right_is_own(which):
+        to_head, extra, source = ext_parts(which)
+        return (4 * extra + head - 1) * 4 + to_head == me
+
+    def ext_start(which, carry):
+        to_head, extra, source = ext_parts(which)
+
+        @pl.when(ext_is_own(which))
+        def _():
+            pltpu.make_async_copy(send_ref.at[source], qkv.at[:, pl.ds(11, 2), tile], ext_recv.at[tile]).start()
+
+        @pl.when(jnp.logical_not(ext_is_own(which)))
+        def _():
+            ext_copy(which).start()
+
+        @pl.when(head < 3)
+        def _():
+            @pl.when(left_is_own(which))
+            def _():
+                pltpu.make_async_copy(send_ref.at[source, pl.ds(1, 2), 1], qkv.at[pl.ds(1, 2), 10, tile],
+                                      left_recv.at[tile]).start()
+
+            @pl.when(jnp.logical_not(left_is_own(which)))
+            def _():
+                left_copy(which).start()
+
+        @pl.when(head > 0)
+        def _():
+            @pl.when(right_is_own(which))
+            def _():
+                pltpu.make_async_copy(send_ref.at[source, pl.ds(1, 2), 0], qkv.at[pl.ds(1, 2), 13, tile],
+                                      right_recv.at[tile]).start()
+
+            @pl.when(jnp.logical_not(right_is_own(which)))
+            def _():
+                right_copy(which).start()
+
+        return carry
+
+    lax.fori_loop(0, 8, ext_start, 0)
+
+    blank = jnp.zeros((FRAMES, 32, HEAD_DIM), jnp.bfloat16)
+    for part in (1, 2):
+        qkv[part, 0] = blank
+        qkv[part, 9] = blank
+
+        @pl.when(col == 0)
+        def _(part=part):
+            qkv[part, 10] = blank
+
+        @pl.when(col == 3)
+        def _(part=part):
+            qkv[part, 13] = blank
+
+    acc[...] = jnp.zeros_like(acc)
+
+    def main_arrive(other, carry):
+        landing(qkv.at[:, pl.ds(1 + 2 * (other % 4), 2), other // 4], main_recv.at[other]).wait()
+        return carry
+
+    lax.fori_loop(0, 32, main_arrive, 0)
+
+    def up_arrive(other, carry):
+        landing(gbuf.at[pl.ds(1 + 2 * (other % 4), 2), :, pl.ds(16 * (other // 4), 16)], up_recv.at[other]).wait()
+        return carry
+
+    lax.fori_loop(0, 8, up_arrive, 0)
+    for half in range(2):
+        landing(gbuf.at[pl.ds(11, 2), :, pl.ds(16 * half, 16)], upx_recv.at[half]).wait()
+
+    def ext_arrive(frame, carry):
+        landing(qkv.at[:, pl.ds(11, 2), frame], ext_recv.at[frame]).wait()
+
+        @pl.when(col > 0)
+        def _():
+            landing(qkv.at[pl.ds(1, 2), 10, frame], left_recv.at[frame]).wait()
+
+        @pl.when(col < 3)
+        def _():
+            landing(qkv.at[pl.ds(1, 2), 13, frame], right_recv.at[frame]).wait()
+
+        return carry
+
+    lax.fori_loop(0, 8, ext_arrive, 0)
+
+    scaling = HEAD_DIM ** (-0.5)
+    key_at = lax.broadcasted_iota(jnp.int32, (768, 1), 0)
+
+    def one_tile(job, carry):
+        first = job + 2 * (job // 8)
+        low = jnp.where((job == 0) | ((job == 8) & (col == 0)), 256, 0)
+        high = jnp.where((job == 7) | ((job == 9) & (col == 3)), 512, 768)
+        usable = (key_at >= low) & (key_at < high)
+        bias = jnp.where(usable, 0.0, -1e30)
+        query = qkv[0, first + 1].reshape(256, HEAD_DIM)
+        grad = gbuf[first + 1].reshape(256, HEAD_DIM)
+        keys = qkv[1, pl.ds(first, 3)].reshape(768, HEAD_DIM)
+        values = qkv[2, pl.ds(first, 3)].reshape(768, HEAD_DIM)
+        scores = lax.dot_general(keys, query, (((1,), (1,)), ((), ())), preferred_element_type=jnp.float32)
+        scores = scores * (scaling * math.log2(math.e)) + bias
+        highest = jnp.max(scores, axis=0, keepdims=True)
+        raised = jnp.exp2(scores - highest)
+        weights = raised * (1.0 / jnp.sum(raised, axis=0, keepdims=True))
+        weights_low = weights.astype(jnp.bfloat16)
+        mixed = lax.dot_general(values, weights_low, (((0,), (0,)), ((), ())), preferred_element_type=jnp.float32)
+        grad_across = grad.astype(jnp.float32).T
+        offsets = jnp.sum(grad_across * mixed, axis=0, keepdims=True)
+        weight_grad = lax.dot_general(values, grad, (((1,), (1,)), ((), ())), preferred_element_type=jnp.float32)
+        score_low = (weights * (weight_grad - offsets)).astype(jnp.bfloat16)
+        query_grad = lax.dot_general(keys, score_low, (((0,), (0,)), ((), ())), preferred_element_type=jnp.float32)
+        obuf[0, first + 1] = mixed.T.astype(jnp.bfloat16).reshape(FRAMES, 32, HEAD_DIM)
+        obuf[1, first + 1] = (query_grad * scaling).T.astype(jnp.bfloat16).reshape(FRAMES, 32, HEAD_DIM)
+        key_terms = lax.dot_general(score_low, query, (((1,), (0,)), ((), ())), preferred_element_type=jnp.float32)
+        value_terms = lax.dot_general(weights_low, grad, (((1,), (0,)), ((), ())), preferred_element_type=jnp.float32)
+        acc[0, pl.ds(first, 3)] += (key_terms * scaling).reshape(3, 256, HEAD_DIM)
+        acc[1, pl.ds(first, 3)] += value_terms.reshape(3, 256, HEAD_DIM)
+        return carry
+
+    lax.fori_loop(0, 10, one_tile, 0)
+
+    def settle_slot(slot, carry):
+        for part in range(2):
+            obuf[2 + part, slot] = acc[part, slot].astype(jnp.bfloat16).reshape(FRAMES, 32, HEAD_DIM)
+        return carry
+
+    lax.fori_loop(1, SLOTS, settle_slot, 0)
+
+    def out_parts(other):
+        return obuf.at[:, pl.ds(1 + 2 * (other % 4), 2), :, pl.ds(16 * (other // 4), 16)]
+
+    def out_copy(other):
+        return push(out_parts(other), landed.at[:, tile], out_send.at[other], out_recv.at[tile], other, head)
+
+    def out_start(step, carry):
+        out_copy((tile + step) % 8).start()
+        return carry
+
+    lax.fori_loop(1, 8, out_start, 0)
+    pltpu.make_async_copy(out_parts(tile), landed.at[:, tile], out_recv.at[tile]).start()
+
+    def outx_copy(half):
+        return push(obuf.at[:, pl.ds(11, 2), :, pl.ds(16 * half, 16)], landed.at[:, 8 + row_half],
+                    outx_send.at[half], outx_recv.at[row_half], 4 * half + col, head)
+
+    def rim_copy(half, side):
+        slot, step = ((13, 1), (10, -1))[side]
+        return push(obuf.at[pl.ds(2, 2), slot, :, pl.ds(16 * half, 16)], rims.at[row_half, side],
+                    rim_send.at[half, side], rim_recv.at[row_half, side], 4 * half + col + step, head)
+
+    for half in range(2):
+        @pl.when(row_half == half)
+        def _(half=half):
+            pltpu.make_async_copy(obuf.at[:, pl.ds(11, 2), :, pl.ds(16 * half, 16)], landed.at[:, 8 + row_half],
+                                  outx_recv.at[row_half]).start()
+
+        @pl.when(row_half != half)
+        def _(half=half):
+            outx_copy(half).start()
+
+        @pl.when(col < 3)
+        def _(half=half):
+            rim_copy(half, 0).start()
+
+        @pl.when(col > 0)
+        def _(half=half):
+            rim_copy(half, 1).start()
+
+    for extra in range(2):
+        @pl.when(col == 0)
+        def _(extra=extra):
+            rims[extra, 0] = jnp.zeros((2, FRAMES, 16, HEAD_DIM), jnp.bfloat16)
+
+        @pl.when(col == 3)
+        def _(extra=extra):
+            rims[extra, 1] = jnp.zeros((2, FRAMES, 16, HEAD_DIM), jnp.bfloat16)
+
+    def out_arrive(other, carry):
+        landing(landed.at[:, other], out_recv.at[other]).wait()
+        for part in range(4):
+            out_ref[part, other] = landed[part, other]
+        return carry
+
+    lax.fori_loop(0, 8, out_arrive, 0)
+    for extra in range(2):
+        landing(landed.at[:, 8 + extra], outx_recv.at[extra]).wait()
+
+        @pl.when(col > 0)
+        def _(extra=extra):
+            landing(rims.at[extra, 0], rim_recv.at[extra, 0]).wait()
+
+        @pl.when(col < 3)
+        def _(extra=extra):
+            landing(rims.at[extra, 1], rim_recv.at[extra, 1]).wait()
+
+        for part in range(2):
+            out_ref[part, 8 + extra] = landed[part, 8 + extra]
+            for side in range(2):
+                total = landed[2 + part, 8 + extra, side].astype(jnp.float32)
+                total = total + rims[extra, side, part].astype(jnp.float32)
+                out_ref[2 + part, 8 + extra, side] = total.astype(jnp.bfloat16)
+
+    def main_left(step, carry):
+        main_copy((me + step) % 32).wait_send()
+        return carry
+
+    lax.fori_loop(1, 32, main_left, 0)
+
+    def group_left(step, carry):
+        up_copy((tile + step) % 8).wait_send()
+        out_copy((tile + step) % 8).wait_send()
+        return carry
+
+    lax.fori_loop(1, 8, group_left, 0)
+
+    def ext_left(which, carry):
+        @pl.when(jnp.logical_not(ext_is_own(which)))
+        def _():
+            ext_copy(which).wait_send()
+
+        @pl.when((head < 3) & jnp.logical_not(left_is_own(which)))
+        def _():
+            left_copy(which).wait_send()
+
+        @pl.when((head > 0) & jnp.logical_not(right_is_own(which)))
+        def _():
+            right_copy(which).wait_send()
+
+        return carry
+
+    lax.fori_loop(0, 8, ext_left, 0)
+    for half in range(2):
+        @pl.when(row_half != half)
+        def _(half=half):
+            upx_copy(half).wait_send()
+            outx_copy(half).wait_send()
+
+        @pl.when(col < 3)
+        def _(half=half):
+            rim_copy(half, 0).wait_send()
+
+        @pl.when(col > 0)
+        def _(half=half):
+            rim_copy(half, 1).wait_send()
+
+
+def fast_local(query_slab, key_slab, value_slab, upstream):
+    def by_head(slab):
+        shaped = slab.reshape(4, 2, 2, 4, 40, HEAD_DIM).transpose(4, 2, 1, 0, 3, 5)
+        return shaped.reshape(40, 2, 32, HEAD_DIM)
+
+    send = jnp.stack((by_head(query_slab), by_head(key_slab), by_head(value_slab)), axis=1)
+    up = upstream.reshape(FRAMES, 4, 2, 4, 10, HEAD_DIM).transpose(4, 2, 0, 1, 3, 5)
+    up = up.reshape(10, 2, FRAMES, 16, HEAD_DIM)
+    dma = pltpu.SemaphoreType.DMA
+    out = pl.pallas_call(
+        fast_kernel,
+        out_shape=jax.ShapeDtypeStruct((4, 10, 2, FRAMES, 16, HEAD_DIM), jnp.bfloat16),
+        in_specs=[pl.BlockSpec(memory_space=pltpu.VMEM)] * 2,
+        out_specs=pl.BlockSpec(memory_space=pltpu.VMEM),
+        scratch_shapes=[
+            pltpu.VMEM((3, SLOTS, FRAMES, 32, HEAD_DIM), jnp.bfloat16),
+            pltpu.VMEM((SLOTS, FRAMES, 32, HEAD_DIM), jnp.bfloat16),
+            pltpu.VMEM((4, SLOTS, FRAMES, 32, HEAD_DIM), jnp.bfloat16),
+            pltpu.VMEM((2, SLOTS, 256, HEAD_DIM), jnp.float32),
+            pltpu.VMEM((4, 10, 2, FRAMES, 16, HEAD_DIM), jnp.bfloat16),
+            pltpu.VMEM((2, 2, 2, FRAMES, 16, HEAD_DIM), jnp.bfloat16),
+            dma((32,)), dma((32,)), dma((8,)), dma((8,)), dma((8,)), dma((8,)), dma((8,)), dma((8,)),
+            dma((8,)), dma((8,)), dma((2,)), dma((2,)), dma((8,)), dma((8,)), dma((2,)), dma((2,)),
+            dma((2, 2)), dma((2, 2)),
+        ],
+        compiler_params=pltpu.CompilerParams(
+            collective_id=0, has_side_effects=True, vmem_limit_bytes=48 * 1024 * 1024
+        ),
+        cost_estimate=pl.CostEstimate(flops=3 * 10**9, bytes_accessed=8 * 10**6, transcendentals=2 * 10**6),
+    )(send, up)
+    out = out.reshape(4, 10, 2, FRAMES, 4, 4, HEAD_DIM).transpose(0, 3, 4, 2, 5, 1, 6).reshape(4, 256, 1280)
+    return (out[0], out[1], out[2], out[3])
+
+
 def solution(mesh):
     placed = (
         P("tile", None, "head", None),
@@ -237,8 +620,14 @@
         P("tile", None, "head", None),
         P("tile", "head"),
     )
+
+    def chosen(query_slab, key_slab, value_slab, upstream):
+        two_rows = query_slab.shape == (4, 2, 8, 40 * HEAD_DIM) and upstream.shape == (256, 10 * HEAD_DIM)
+        body = fast_local if two_rows and mesh.shape["tile"] == 8 and mesh.shape["head"] == 4 else local
+        return body(query_slab, key_slab, value_slab, upstream)
+
     return jax.shard_map(
-        local,
+        chosen,
         mesh=mesh,
         in_specs=placed,
         out_specs=(P("tile", "head"), P("tile", "head"), P("tile", "head"), P("tile", "head")),

time: 853 us -> 161 us (0.19); the launches traced: 836 us -> 159 us
  local copies, waits for them, and re-layouts: 421 us -> 12.3 us
  waiting for transfers between devices: 189 us -> 0 us
  Pallas kernels: 0 us -> 146 us
  other arithmetic: 75.1 us -> 0.21 us
  starting transfers between devices: 46.1 us -> 0 us
  blocking collectives: 36.8 us -> 0 us
  loops' own time: 33.9 us -> 0 us
  matrix products: 33 us -> 0 us
    pallas_call x0 -> x1, Pallas kernels: none -> 146 us  [fast_local(): pl.pallas_call(fast_kernel, out_shape=jax.ShapeDtypeStruct((4, 10, 2, FRA...]
    ppermute x8 -> x0, waiting for transfers between devices: 141 us -> none  [from_behind(): lax.ppermute(value, axis, [(source, source + steps) for source in range(l...]
    unnamed x19 -> x7, local copies, waits for them, and re-layouts: 116 us -> 1.7 us
    another operation x24 -> x0, local copies, waits for them, and re-layouts: 64.5 us -> none
    transpose x8 -> x1, local copies, waits for them, and re-layouts: 57.4 us -> 0.32 us  [fast_local(): upstream.reshape(FRAMES, 4, 2, 4, 10, HEAD_DIM).transpose(4, 2, 0, 1, 3, 5)]
    while x83 -> x0, local copies, waits for them, and re-layouts: 55 us -> none  [the longest x7 43.1 us: local(): lax.scan(one_column, totals, jnp.arange(tile_cols, dtype=jnp.int32))]
    all_to_all x4 -> x0, waiting for transfers between devices: 48 us -> none  [the longest x1 48 us: local(): lax.all_to_all(to_owners(query_rows), 'tile', split_axis=0, concat_axis=1...]
    all_to_all x2 -> x0, blocking collectives: 36.8 us -> none  [the longest x1 24 us: local(): lax.all_to_all(to_owners(value_rows), 'tile', split_axis=0, concat_axis=1...]
  transfers between devices with their start and end apart: 12 -> 0, of which waited for: 5 -> 0; matrix products, arithmetic and copies ran while one was open for 19% -> 0% of each run, Pallas kernels for 0% -> 0%
where the time goes in v1:
time: 161 us; the launch traced here: 159 us
  Pallas kernels  146 us (91%)
  local copies, waits for them, and re-layouts  12.3 us (8%)
    pallas_call x1, Pallas kernels, fast_local(): pl.pallas_call(fast_kernel, out_shape=jax.ShapeDtypeStruct((4, 10, 2, FRA...  146 us
    reshape x1, local copies, waits for them, and re-layouts, fast_local(): out.reshape(4, 10, 2, FRAMES, 4, 4, HEAD_DIM).transpose(0, 3, 4, 2, 5, 1, 6)  3.24 us

profile of v1, /device:TPU:0, one launch (start us, length us, event | category | flops | bytes accessed | tf_op | source)
XLA Modules:
  0.0 159.0 jit_solution(17610639778345038729)
XLA Ops:
  0.6 0.0 copy-start
  0.6 1.3 copy.21
  1.9 0.0 copy-start.1
  1.9 0.3 copy.16
  2.3 0.0 copy-done
  2.3 0.1 copy.22
  2.4 0.3 copy.17
  2.7 0.3 copy-done.1
  3.0 0.1 copy.23
  3.1 0.3 copy.18
  3.4 0.2 pad_maximum_fusion.send_ref
  3.7 1.5 reshape.38
  5.1 0.3 copy.19
  5.5 145.7 %shard_map.75 = bf16[4,10,2,8,16,128]{5,4,3,2,1,0:T(8,128)(2,1)S(1)} custom-call(bf16[40,3,2,32,128]{4,3,2,1,0:T(8,128)(2,1)S(1)} %pad_maximum_fusion.send_ref, bf16[10,2,8,16,128]{4,3,2,1,0:T(8,128)(2,1)S(1)} %bitcast.47), custom_call_target="tpu_custom_call" | custom-call | flops 3000000000 | bytes 8000000 | tf_op jit(solution)/shard_map/pallas_call | solution.py:591
  151.1 3.2 %copy.33 = bf16[4,10,2,8,4,4,128]{6,1,5,2,4,3,0:T(8,128)(2,1)S(1)} copy(bf16[4,10,2,8,4,4,128]{6,5,4,3,2,1,0:T(4,128)(2,1)S(1)} %bitcast.46) | data formatting | bytes 5242880 | tf_op jit(solution)/shard_map/reshape | solution.py:612
  154.4 1.8 %fusion = (bf16[1,8,4,2,4,10,128]{6,5,4,3,2,1,0:T(8,128)(2,1)S(1)}, bf16[1,8,4,2,4,10,128]{6,5,4,3,2,1,0:T(8,128)(2,1)S(1)}, bf16[1,8,4,2,4,10,128]{6,5,4,3,2,1,...) fusion(bf16[4,8,4,2,4,10,128]{6,5,4,3,2,1,0:T(8,128)(2,1)S(1)} %bitcast.48), kind=kLoop, calls=%fused_computation.6 | loop fusion | bytes 5242880 | tf_op jit(solution)/shard_map/slice | solution.py:613
  156.2 1.4 copy_bitcast_fusion.1
  157.6 1.4 copy_bitcast_fusion.3
Async XLA Ops:
  0.6 1.6 %copy-start = (bf16[4,2,8,5120]{3,2,1,0:T(8,128)(2,1)S(1)}, bf16[4,2,8,5120]{3,2,1,0:T(8,128)(2,1)}, u32[]{:S(2)}) copy-start(bf16[4,2,8,5120]{3,2,1,0:T(8,128)(2,1)} %param.5) | copy-start | bytes 1966084
  1.9 1.1 copy-start.1

commit v2 on v1

--- a/solution.py
+++ b/solution.py
@@ -238,7 +238,7 @@
 SLOTS = 14
 
 
-def fast_kernel(send_ref, up_ref, out_ref, qkv, gbuf, obuf, acc, landed, rims,
+def fast_kernel(send_ref, up_ref, attended_ref, query_ref, key_ref, value_ref, qkv, gbuf, obuf, acc, landed, rims,
                 main_send, main_recv, ext_send, ext_recv, left_send, left_recv, right_send, right_recv,
                 up_send, up_recv, upx_send, upx_recv, out_send, out_recv, outx_send, outx_recv,
                 rim_send, rim_recv):
@@ -266,114 +266,120 @@
     def landing(dst, recv_sem):
         return pltpu.make_async_copy(dst, dst, recv_sem)
 
+    rows = pl.ds(16 * row_half, 16)
+
+    def ext_parts(which):
+        to_head, extra = which // 2, which % 2
+        return to_head, extra, to_head * 10 + 8 + extra
+
+    def ext_copy(which):
+        to_head, extra, source = ext_parts(which)
+        return push(send_ref.at[source], qkv.at[:, pl.ds(11, 2), tile],
+                    ext_send.at[which], ext_recv.at[tile], 4 * extra + head, to_head)
+
+    def ext_is_own(which):
+        to_head, extra, source = ext_parts(which)
+        return (4 * extra + head) * 4 + to_head == me
+
+    def left_copy(which):
+        to_head, extra, source = ext_parts(which)
+        return push(send_ref.at[source, pl.ds(1, 2), 1], qkv.at[pl.ds(1, 2), 10, tile],
+                    left_send.at[which], left_recv.at[tile], 4 * extra + head + 1, to_head)
+
+    def left_is_own(which):
+        to_head, extra, source = ext_parts(which)
+        return (4 * extra + head + 1) * 4 + to_head == me
+
+    def right_copy(which):
+        to_head, extra, source = ext_parts(which)
+        return push(send_ref.at[source, pl.ds(1, 2), 0], qkv.at[pl.ds(1, 2), 13, tile],
+                    right_send.at[which], right_recv.at[tile], 4 * extra + head - 1, to_head)
+
+    def right_is_own(which):
+        to_head, extra, source = ext_parts(which)
+        return (4 * extra + head - 1) * 4 + to_head == me
+
+    def ext_start(which, carry):
+        to_head, extra, source = ext_parts(which)
+
+        @pl.when(ext_is_own(which))
+        def _():
+            pltpu.make_async_copy(send_ref.at[source], qkv.at[:, pl.ds(11, 2), tile], ext_recv.at[tile]).start()
+
+        @pl.when(jnp.logical_not(ext_is_own(which)))
+        def _():
+            ext_copy(which).start()
+
+        @pl.when(head < 3)
+        def _():
+            @pl.when(left_is_own(which))
+            def _():
+                pltpu.make_async_copy(send_ref.at[source, pl.ds(1, 2), 1], qkv.at[pl.ds(1, 2), 10, tile],
+                                      left_recv.at[tile]).start()
+
+            @pl.when(jnp.logical_not(left_is_own(which)))
+            def _():
+                left_copy(which).start()
+
+        @pl.when(head > 0)
+        def _():
+            @pl.when(right_is_own(which))
+            def _():
+                pltpu.make_async_copy(send_ref.at[source, pl.ds(1, 2), 0], qkv.at[pl.ds(1, 2), 13, tile],
+                                      right_recv.at[tile]).start()
+
+            @pl.when(jnp.logical_not(right_is_own(which)))
+            def _():
+                right_copy(which).start()
+
+        return carry
+
+    lax.fori_loop(0, 8, ext_start, 0)
+
+    def upx_copy(extra):
+        return push(up_ref.at[8 + extra], gbuf.at[pl.ds(11, 2), :, rows],
+                    upx_send.at[extra], upx_recv.at[row_half], 4 * extra + col, head)
+
+    for extra in range(2):
+        @pl.when(row_half == extra)
+        def _(extra=extra):
+            pltpu.make_async_copy(up_ref.at[8 + extra], gbuf.at[pl.ds(11, 2), :, rows],
+                                  upx_recv.at[row_half]).start()
+
+        @pl.when(row_half != extra)
+        def _(extra=extra):
+            upx_copy(extra).start()
+
+    def up_copy(other):
+        return push(up_ref.at[other], gbuf.at[pl.ds(1 + 2 * col, 2), :, rows],
+                    up_send.at[other], up_recv.at[tile], other, head)
+
+    def up_start(step, carry):
+        up_copy((tile + 3 + step + step // 5) % 8).start()
+        return carry
+
+    lax.fori_loop(1, 8, up_start, 0)
+    pltpu.make_async_copy(up_ref.at[tile], gbuf.at[pl.ds(1 + 2 * col, 2), :, rows], up_recv.at[tile]).start()
+
     def main_copy(other):
         to_tile, to_head = other // 4, other % 4
         src = send_ref.at[to_head * 10 + to_tile]
         dst = qkv.at[:, pl.ds(1 + 2 * head, 2), tile]
         return push(src, dst, main_send.at[other], main_recv.at[me], to_tile, to_head)
 
-    def main_start(step, carry):
-        main_copy((me + step) % 32).start()
-        return carry
-
-    lax.fori_loop(1, 32, main_start, 0)
+    def main_peer(place):
+        turn = place // 4
+        shift = 12 + ((turn + 1) // 2) * (2 * (turn % 2) - 1)
+        return ((tile + shift) % 8) * 4 + (head + place) % 4
+
+    def main_start(place, carry):
+        main_copy(main_peer(place)).start()
+        return carry
+
+    lax.fori_loop(0, 28, main_start, 0)
+    lax.fori_loop(29, 32, main_start, 0)
     pltpu.make_async_copy(send_ref.at[head * 10 + tile], qkv.at[:, pl.ds(1 + 2 * head, 2), tile],
                           main_recv.at[me]).start()
-
-    rows = pl.ds(16 * row_half, 16)
-
-    def up_copy(other):
-        return push(up_ref.at[other], gbuf.at[pl.ds(1 + 2 * col, 2), :, rows],
-                    up_send.at[other], up_recv.at[tile], other, head)
-
-    def up_start(step, carry):
-        up_copy((tile + step) % 8).start()
-        return carry
-
-    lax.fori_loop(1, 8, up_start, 0)
-    pltpu.make_async_copy(up_ref.at[tile], gbuf.at[pl.ds(1 + 2 * col, 2), :, rows], up_recv.at[tile]).start()
-
-    def upx_copy(extra):
-        return push(up_ref.at[8 + extra], gbuf.at[pl.ds(11, 2), :, rows],
-                    upx_send.at[extra], upx_recv.at[row_half], 4 * extra + col, head)
-
-    for extra in range(2):
-        @pl.when(row_half == extra)
-        def _(extra=extra):
-            pltpu.make_async_copy(up_ref.at[8 + extra], gbuf.at[pl.ds(11, 2), :, rows],
-                                  upx_recv.at[row_half]).start()
-
-        @pl.when(row_half != extra)
-        def _(extra=extra):
-            upx_copy(extra).start()
-
-    def ext_parts(which):
-        to_head, extra = which // 2, which % 2
-        return to_head, extra, to_head * 10 + 8 + extra
-
-    def ext_copy(which):
-        to_head, extra, source = ext_parts(which)
-        return push(send_ref.at[source], qkv.at[:, pl.ds(11, 2), tile],
-                    ext_send.at[which], ext_recv.at[tile], 4 * extra + head, to_head)
-
-    def ext_is_own(which):
-        to_head, extra, source = ext_parts(which)
-        return (4 * extra + head) * 4 + to_head == me
-
-    def left_copy(which):
-        to_head, extra, source = ext_parts(which)
-        return push(send_ref.at[source, pl.ds(1, 2), 1], qkv.at[pl.ds(1, 2), 10, tile],
-                    left_send.at[which], left_recv.at[tile], 4 * extra + head + 1, to_head)
-
-    def left_is_own(which):
-        to_head, extra, source = ext_parts(which)
-        return (4 * extra + head + 1) * 4 + to_head == me
-
-    def right_copy(which):
-        to_head, extra, source = ext_parts(which)
-        return push(send_ref.at[source, pl.ds(1, 2), 0], qkv.at[pl.ds(1, 2), 13, tile],
-                    right_send.at[which], right_recv.at[tile], 4 * extra + head - 1, to_head)
-
-    def right_is_own(which):
-        to_head, extra, source = ext_parts(which)
-        return (4 * extra + head - 1) * 4 + to_head == me
-
-    def ext_start(which, carry):
-        to_head, extra, source = ext_parts(which)
-
-        @pl.when(ext_is_own(which))
-        def _():
-            pltpu.make_async_copy(send_ref.at[source], qkv.at[:, pl.ds(11, 2), tile], ext_recv.at[tile]).start()
-
-        @pl.when(jnp.logical_not(ext_is_own(which)))
-        def _():
-            ext_copy(which).start()
-
-        @pl.when(head < 3)
-        def _():
-            @pl.when(left_is_own(which))
-            def _():
-                pltpu.make_async_copy(send_ref.at[source, pl.ds(1, 2), 1], qkv.at[pl.ds(1, 2), 10, tile],
-                                      left_recv.at[tile]).start()
-
-            @pl.when(jnp.logical_not(left_is_own(which)))
-            def _():
-                left_copy(which).start()
-
-        @pl.when(head > 0)
-        def _():
-            @pl.when(right_is_own(which))
-            def _():
-                pltpu.make_async_copy(send_ref.at[source, pl.ds(1, 2), 0], qkv.at[pl.ds(1, 2), 13, tile],
-                                      right_recv.at[tile]).start()
-
-            @pl.when(jnp.logical_not(right_is_own(which)))
-            def _():
-                right_copy(which).start()
-
-        return carry
-
-    lax.fori_loop(0, 8, ext_start, 0)
 
     blank = jnp.zeros((FRAMES, 32, HEAD_DIM), jnp.bfloat16)
     for part in (1, 2):
@@ -390,39 +396,10 @@
 
     acc[...] = jnp.zeros_like(acc)
 
-    def main_arrive(other, carry):
-        landing(qkv.at[:, pl.ds(1 + 2 * (other % 4), 2), other // 4], main_recv.at[other]).wait()
-        return carry
-
-    lax.fori_loop(0, 32, main_arrive, 0)
-
-    def up_arrive(other, carry):
-        landing(gbuf.at[pl.ds(1 + 2 * (other % 4), 2), :, pl.ds(16 * (other // 4), 16)], up_recv.at[other]).wait()
-        return carry
-
-    lax.fori_loop(0, 8, up_arrive, 0)
-    for half in range(2):
-        landing(gbuf.at[pl.ds(11, 2), :, pl.ds(16 * half, 16)], upx_recv.at[half]).wait()
-
-    def ext_arrive(frame, carry):
-        landing(qkv.at[:, pl.ds(11, 2), frame], ext_recv.at[frame]).wait()
-
-        @pl.when(col > 0)
-        def _():
-            landing(qkv.at[pl.ds(1, 2), 10, frame], left_recv.at[frame]).wait()
-
-        @pl.when(col < 3)
-        def _():
-            landing(qkv.at[pl.ds(1, 2), 13, frame], right_recv.at[frame]).wait()
-
-        return carry
-
-    lax.fori_loop(0, 8, ext_arrive, 0)
-
     scaling = HEAD_DIM ** (-0.5)
     key_at = lax.broadcasted_iota(jnp.int32, (768, 1), 0)
 
-    def one_tile(job, carry):
+    def one_tile(job):
         first = job + 2 * (job // 8)
         low = jnp.where((job == 0) | ((job == 8) & (col == 0)), 256, 0)
         high = jnp.where((job == 7) | ((job == 9) & (col == 3)), 512, 768)
@@ -450,29 +427,30 @@
         value_terms = lax.dot_general(weights_low, grad, (((1,), (0,)), ((), ())), preferred_element_type=jnp.float32)
         acc[0, pl.ds(first, 3)] += (key_terms * scaling).reshape(3, 256, HEAD_DIM)
         acc[1, pl.ds(first, 3)] += value_terms.reshape(3, 256, HEAD_DIM)
-        return carry
-
-    lax.fori_loop(0, 10, one_tile, 0)
-
-    def settle_slot(slot, carry):
+
+    def settle(slot):
         for part in range(2):
             obuf[2 + part, slot] = acc[part, slot].astype(jnp.bfloat16).reshape(FRAMES, 32, HEAD_DIM)
-        return carry
-
-    lax.fori_loop(1, SLOTS, settle_slot, 0)
-
-    def out_parts(other):
-        return obuf.at[:, pl.ds(1 + 2 * (other % 4), 2), :, pl.ds(16 * (other // 4), 16)]
-
-    def out_copy(other):
-        return push(out_parts(other), landed.at[:, tile], out_send.at[other], out_recv.at[tile], other, head)
-
-    def out_start(step, carry):
-        out_copy((tile + step) % 8).start()
-        return carry
-
-    lax.fori_loop(1, 8, out_start, 0)
-    pltpu.make_async_copy(out_parts(tile), landed.at[:, tile], out_recv.at[tile]).start()
+
+    def out_piece(pair, other):
+        return obuf.at[pl.ds(2 * pair, 2), pl.ds(1 + 2 * (other % 4), 2), :, pl.ds(16 * (other // 4), 16)]
+
+    def out_copy(pair, other):
+        return push(out_piece(pair, other), landed.at[pl.ds(2 * pair, 2), tile],
+                    out_send.at[pair, other], out_recv.at[pair, tile], other, head)
+
+    def out_start(pair, column):
+        for step in (1, 0):
+            other = 4 * ((row_half + step) % 2) + column
+
+            @pl.when(other == tile)
+            def _(other=other):
+                pltpu.make_async_copy(out_piece(pair, other), landed.at[pl.ds(2 * pair, 2), tile],
+                                      out_recv.at[pair, tile]).start()
+
+            @pl.when(other != tile)
+            def _(other=other):
+                out_copy(pair, other).start()
 
     def outx_copy(half):
         return push(obuf.at[:, pl.ds(11, 2), :, pl.ds(16 * half, 16)], landed.at[:, 8 + row_half],
@@ -483,6 +461,31 @@
         return push(obuf.at[pl.ds(2, 2), slot, :, pl.ds(16 * half, 16)], rims.at[row_half, side],
                     rim_send.at[half, side], rim_recv.at[row_half, side], 4 * half + col + step, head)
 
+    def ext_arrive(frame, carry):
+        landing(qkv.at[:, pl.ds(11, 2), frame], ext_recv.at[frame]).wait()
+
+        @pl.when(col > 0)
+        def _():
+            landing(qkv.at[pl.ds(1, 2), 10, frame], left_recv.at[frame]).wait()
+
+        @pl.when(col < 3)
+        def _():
+            landing(qkv.at[pl.ds(1, 2), 13, frame], right_recv.at[frame]).wait()
+
+        return carry
+
+    lax.fori_loop(0, 8, ext_arrive, 0)
+
+    for half in range(2):
+        landing(gbuf.at[pl.ds(11, 2), :, pl.ds(16 * half, 16)], upx_recv.at[half]).wait()
+
+    def ext_tile(job, carry):
+        one_tile(job)
+        return carry
+
+    lax.fori_loop(8, 10, ext_tile, 0)
+    for slot in range(10, SLOTS):
+        settle(slot)
     for half in range(2):
         @pl.when(row_half == half)
         def _(half=half):
@@ -510,13 +513,54 @@
         def _(extra=extra):
             rims[extra, 1] = jnp.zeros((2, FRAMES, 16, HEAD_DIM), jnp.bfloat16)
 
-    def out_arrive(other, carry):
-        landing(landed.at[:, other], out_recv.at[other]).wait()
-        for part in range(4):
-            out_ref[part, other] = landed[part, other]
-        return carry
-
-    lax.fori_loop(0, 8, out_arrive, 0)
+    def main_arrive(other, carry):
+        landing(qkv.at[:, pl.ds(1 + 2 * (other % 4), 2), other // 4], main_recv.at[other]).wait()
+        return carry
+
+    lax.fori_loop(0, 32, main_arrive, 0)
+
+    def up_arrive(other, carry):
+        landing(gbuf.at[pl.ds(1 + 2 * (other % 4), 2), :, pl.ds(16 * (other // 4), 16)], up_recv.at[other]).wait()
+        return carry
+
+    lax.fori_loop(0, 8, up_arrive, 0)
+    def settle_column(column):
+        settle(1 + 2 * column)
+        settle(2 + 2 * column)
+        out_start(1, column)
+
+    def main_tile(step, carry):
+        one_tile((step + 2 * col) % 8)
+
+        @pl.when(step % 2 == 1)
+        def _():
+            out_start(0, (col + step // 2) % 4)
+
+        @pl.when((step == 4) | (step == 6))
+        def _():
+            settle_column((col + step // 2 - 1) % 4)
+
+        return carry
+
+    lax.fori_loop(0, 8, main_tile, 0)
+    settle_column((col + 3) % 4)
+    settle_column(col)
+
+    upper = lax.broadcasted_iota(jnp.int32, (16, 8, HEAD_DIM), 1) < 4
+
+    def place(ref, which, near, far):
+        near = near.reshape(16, 8, HEAD_DIM)
+        far = far.reshape(16, 8, HEAD_DIM)
+        even = jnp.where(upper, near, pltpu.roll(far, 4, 1))
+        odd = jnp.where(upper, pltpu.roll(near, 4, 1), far)
+        lines = jnp.stack((even, odd), axis=1).reshape(256, HEAD_DIM)
+        ref[:, pl.ds(pl.multiple_of(which * HEAD_DIM, HEAD_DIM), HEAD_DIM)] = lines.astype(jnp.bfloat16)
+
+    out_refs = (attended_ref, query_ref, key_ref, value_ref)
+
+    def wide(part, which, side):
+        return landed[part, which, side].astype(jnp.float32)
+
     for extra in range(2):
         landing(landed.at[:, 8 + extra], outx_recv.at[extra]).wait()
 
@@ -529,11 +573,20 @@
             landing(rims.at[extra, 1], rim_recv.at[extra, 1]).wait()
 
         for part in range(2):
-            out_ref[part, 8 + extra] = landed[part, 8 + extra]
-            for side in range(2):
-                total = landed[2 + part, 8 + extra, side].astype(jnp.float32)
-                total = total + rims[extra, side, part].astype(jnp.float32)
-                out_ref[2 + part, 8 + extra, side] = total.astype(jnp.bfloat16)
+            place(out_refs[part], 8 + extra, wide(part, 8 + extra, 0), wide(part, 8 + extra, 1))
+            place(out_refs[2 + part], 8 + extra,
+                  wide(2 + part, 8 + extra, 0) + rims[extra, 0, part].astype(jnp.float32),
+                  wide(2 + part, 8 + extra, 1) + rims[extra, 1, part].astype(jnp.float32))
+
+    for pair in range(2):
+        def out_arrive(step, carry, pair=pair):
+            other = (tile + step) % 8
+            landing(landed.at[pl.ds(2 * pair, 2), other], out_recv.at[pair, other]).wait()
+            for part in (2 * pair, 2 * pair + 1):
+                place(out_refs[part], other, wide(part, other, 0), wide(part, other, 1))
+            return carry
+
+        lax.fori_loop(0, 8, out_arrive, 0)
 
     def main_left(step, carry):
         main_copy((me + step) % 32).wait_send()
@@ -543,7 +596,8 @@
 
     def group_left(step, carry):
         up_copy((tile + step) % 8).wait_send()
-        out_copy((tile + step) % 8).wait_send()
+        out_copy(0, (tile + step) % 8).wait_send()
+        out_copy(1, (tile + step) % 8).wait_send()
         return carry
 
     lax.fori_loop(1, 8, group_left, 0)
@@ -590,9 +644,9 @@
     dma = pltpu.SemaphoreType.DMA
     out = pl.pallas_call(
         fast_kernel,
-        out_shape=jax.ShapeDtypeStruct((4, 10, 2, FRAMES, 16, HEAD_DIM), jnp.bfloat16),
+        out_shape=[jax.ShapeDtypeStruct((256, 10 * HEAD_DIM), jnp.bfloat16)] * 4,
         in_specs=[pl.BlockSpec(memory_space=pltpu.VMEM)] * 2,
-        out_specs=pl.BlockSpec(memory_space=pltpu.VMEM),
+        out_specs=[pl.BlockSpec(memory_space=pltpu.VMEM)] * 4,
         scratch_shapes=[
             pltpu.VMEM((3, SLOTS, FRAMES, 32, HEAD_DIM), jnp.bfloat16),
             pltpu.VMEM((SLOTS, FRAMES, 32, HEAD_DIM), jnp.bfloat16),
@@ -601,7 +655,7 @@
             pltpu.VMEM((4, 10, 2, FRAMES, 16, HEAD_DIM), jnp.bfloat16),
             pltpu.VMEM((2, 2, 2, FRAMES, 16, HEAD_DIM), jnp.bfloat16),
             dma((32,)), dma((32,)), dma((8,)), dma((8,)), dma((8,)), dma((8,)), dma((8,)), dma((8,)),
-            dma((8,)), dma((8,)), dma((2,)), dma((2,)), dma((8,)), dma((8,)), dma((2,)), dma((2,)),
+            dma((8,)), dma((8,)), dma((2,)), dma((2,)), dma((2, 8)), dma((2, 8)), dma((2,)), dma((2,)),
             dma((2, 2)), dma((2, 2)),
         ],
         compiler_params=pltpu.CompilerParams(
@@ -609,8 +663,7 @@
         ),
         cost_estimate=pl.CostEstimate(flops=3 * 10**9, bytes_accessed=8 * 10**6, transcendentals=2 * 10**6),
     )(send, up)
-    out = out.reshape(4, 10, 2, FRAMES, 4, 4, HEAD_DIM).transpose(0, 3, 4, 2, 5, 1, 6).reshape(4, 256, 1280)
-    return (out[0], out[1], out[2], out[3])
+    return tuple(out)
 
 
 def solution(mesh):

time: 161 us -> 141 us (0.88); the launches traced: 159 us -> 141 us
  Pallas kernels: 146 us -> 132 us
  local copies, waits for them, and re-layouts: 12.3 us -> 7.87 us
    pallas_call x1, Pallas kernels: 146 us -> 132 us  [fast_local(): pl.pallas_call(fast_kernel, out_shape=[jax.ShapeDtypeStruct((256, 10 * HE...]
    unnamed x7 -> x11, local copies, waits for them, and re-layouts: 1.7 us -> 5.05 us
    reshape x1 -> x0, local copies, waits for them, and re-layouts: 3.24 us -> none  [fast_local(): out.reshape(4, 10, 2, FRAMES, 4, 4, HEAD_DIM).transpose(0, 3, 4, 2, 5, 1, 6)]
    squeeze x2 -> x0, local copies, waits for them, and re-layouts: 2.74 us -> none  [fast_local(): return (out[0], out[1], out[2], out[3])]
    slice x1 -> x0, local copies, waits for them, and re-layouts: 1.83 us -> none  [fast_local(): return (out[0], out[1], out[2], out[3])]
where the time goes in v2:
time: 141 us
  Pallas kernels  132 us (94%)
  local copies, waits for them, and re-layouts  7.87 us (6%)
    pallas_call x1, Pallas kernels, fast_local(): pl.pallas_call(fast_kernel, out_shape=[jax.ShapeDtypeStruct((256, 10 * HE...  132 us
    unnamed x11, local copies, waits for them, and re-layouts  5.05 us

profile of v2, /device:TPU:0, one launch (start us, length us, event | category | flops | bytes accessed | tf_op | source)
XLA Modules:
  0.0 141.1 jit_solution(4803641301910836827)
XLA Ops:
  0.6 0.0 copy-start
  0.6 1.3 copy.16
  1.9 0.0 copy-start.1
  1.9 0.3 copy.12
  2.3 0.0 copy-done
  2.3 0.1 copy.17
  2.4 0.3 copy.13
  2.7 0.3 copy-done.1
  3.0 0.1 copy.18
  3.1 0.3 copy.14
  3.4 0.2 pad_maximum_fusion.send_ref
  3.7 1.5 %reshape.26 = bf16[8,4,2,4,10,128]{5,4,3,2,1,0:T(8,128)(2,1)S(1)} reshape(bf16[256,1280]{1,0:T(8,128)(2,1)} %param.7) | data formatting | bytes 1310720 | tf_op jit(solution)/shard_map/reshape | solution.py:642
  5.1 0.3 copy.15
  5.5 132.3 %shard_map.75 = (bf16[256,1280]{1,0:T(8,128)(2,1)S(1)}, bf16[256,1280]{1,0:T(8,128)(2,1)S(1)}, bf16[256,1280]{1,0:T(8,128)(2,1)S(1)}, bf16[256,1280]{1,0:T(8,128)(2,1)S(1)}) custom-call(bf16[40,3,2,32,128]{4,3,2,1,0:T(8,128)(2,1)S(1)} %pad_maximum_fusion.send_ref, bf16[10,2,8,16,128]{4,3,2,1,0:T(8,128)(2,1)S(1)} %bitcast.26), custom_call_target="tpu_custom_call" | custom-call | flops 3000000000 | bytes 8000000 | tf_op jit(solution)/shard_map/pallas_call | solution.py:645
  137.7 0.8 copy.23
  138.6 0.8 copy.24
  139.4 0.8 copy.25
  140.3 0.8 copy.26
Async XLA Ops:
  0.6 1.6 %copy-start = (bf16[4,2,8,5120]{3,2,1,0:T(8,128)(2,1)S(1)}, bf16[4,2,8,5120]{3,2,1,0:T(8,128)(2,1)}, u32[]{:S(2)}) copy-start(bf16[4,2,8,5120]{3,2,1,0:T(8,128)(2,1)} %param.5) | copy-start | bytes 1966084
  1.9 1.1 copy-start.1

commit v3 on v2

--- a/solution.py
+++ b/solution.py
@@ -238,8 +238,9 @@
 SLOTS = 14
 
 
-def fast_kernel(send_ref, up_ref, attended_ref, query_ref, key_ref, value_ref, qkv, gbuf, obuf, acc, landed, rims,
-                main_send, main_recv, ext_send, ext_recv, left_send, left_recv, right_send, right_recv,
+def fast_kernel(query_slab, key_slab, value_slab, grad_in, attended_ref, query_ref, key_ref, value_ref,
+                send_ref, up_ref, qkv, gbuf, obuf, acc, landed, rims,
+                main_send, main_recv, ext_send, ext_recv, side_send, side_recv,
                 up_send, up_recv, upx_send, upx_recv, out_send, out_recv, outx_send, outx_recv,
                 rim_send, rim_recv):
     tile = lax.axis_index("tile")
@@ -256,6 +257,35 @@
         return carry
 
     lax.fori_loop(1, 32, greet, 0)
+
+    def regroup(first, second):
+        upper = lax.broadcasted_iota(jnp.int32, first.shape, first.ndim - 2) < 4
+        near = jnp.where(upper, first, pltpu.roll(second, 4, first.ndim - 2))
+        far = jnp.where(upper, pltpu.roll(first, 4, first.ndim - 2), second)
+        return near, far
+
+    def lanes(which):
+        return pl.ds(pl.multiple_of(which * HEAD_DIM, HEAD_DIM), HEAD_DIM)
+
+    def prepare(which):
+        for part, slab in enumerate((query_slab, key_slab, value_slab)):
+            lines = slab[:, :, :, lanes(which)].astype(jnp.float32).reshape(2, 2, 16, HEAD_DIM)
+            first = lines[:, 0].reshape(4, 8, HEAD_DIM)
+            second = lines[:, 1].reshape(4, 8, HEAD_DIM)
+            for side, taken in enumerate(regroup(first, second)):
+                ordered = jnp.stack((taken[0], taken[2], taken[1], taken[3])).reshape(32, HEAD_DIM)
+                send_ref[which, part, side] = ordered.astype(jnp.bfloat16)
+
+    def prepare_up(which):
+        lines = grad_in[:, lanes(which)].astype(jnp.float32).reshape(16, 2, 8, HEAD_DIM)
+        for side, taken in enumerate(regroup(lines[:, 0], lines[:, 1])):
+            up_ref[which, side] = taken.reshape(FRAMES, 16, HEAD_DIM).astype(jnp.bfloat16)
+
+    def prepare_shared(which, carry):
+        prepare((which // 2) * 10 + 8 + which % 2)
+        return carry
+
+    lax.fori_loop(0, 8, prepare_shared, 0)
     pl.semaphore_wait(barrier, 31)
 
     def push(src, dst, send_sem, recv_sem, to_tile, to_head):
@@ -281,24 +311,6 @@
         to_head, extra, source = ext_parts(which)
         return (4 * extra + head) * 4 + to_head == me
 
-    def left_copy(which):
-        to_head, extra, source = ext_parts(which)
-        return push(send_ref.at[source, pl.ds(1, 2), 1], qkv.at[pl.ds(1, 2), 10, tile],
-                    left_send.at[which], left_recv.at[tile], 4 * extra + head + 1, to_head)
-
-    def left_is_own(which):
-        to_head, extra, source = ext_parts(which)
-        return (4 * extra + head + 1) * 4 + to_head == me
-
-    def right_copy(which):
-        to_head, extra, source = ext_parts(which)
-        return push(send_ref.at[source, pl.ds(1, 2), 0], qkv.at[pl.ds(1, 2), 13, tile],
-                    right_send.at[which], right_recv.at[tile], 4 * extra + head - 1, to_head)
-
-    def right_is_own(which):
-        to_head, extra, source = ext_parts(which)
-        return (4 * extra + head - 1) * 4 + to_head == me
-
     def ext_start(which, carry):
         to_head, extra, source = ext_parts(which)
 
@@ -309,28 +321,6 @@
         @pl.when(jnp.logical_not(ext_is_own(which)))
         def _():
             ext_copy(which).start()
-
-        @pl.when(head < 3)
-        def _():
-            @pl.when(left_is_own(which))
-            def _():
-                pltpu.make_async_copy(send_ref.at[source, pl.ds(1, 2), 1], qkv.at[pl.ds(1, 2), 10, tile],
-                                      left_recv.at[tile]).start()
-
-            @pl.when(jnp.logical_not(left_is_own(which)))
-            def _():
-                left_copy(which).start()
-
-        @pl.when(head > 0)
-        def _():
-            @pl.when(right_is_own(which))
-            def _():
-                pltpu.make_async_copy(send_ref.at[source, pl.ds(1, 2), 0], qkv.at[pl.ds(1, 2), 13, tile],
-                                      right_recv.at[tile]).start()
-
-            @pl.when(jnp.logical_not(right_is_own(which)))
-            def _():
-                right_copy(which).start()
 
         return carry
 
@@ -341,6 +331,8 @@
                     upx_send.at[extra], upx_recv.at[row_half], 4 * extra + col, head)
 
     for extra in range(2):
+        prepare_up(8 + extra)
+
         @pl.when(row_half == extra)
         def _(extra=extra):
             pltpu.make_async_copy(up_ref.at[8 + extra], gbuf.at[pl.ds(11, 2), :, rows],
@@ -355,10 +347,13 @@
                     up_send.at[other], up_recv.at[tile], other, head)
 
     def up_start(step, carry):
-        up_copy((tile + 3 + step + step // 5) % 8).start()
+        other = (tile + 3 + step + step // 5) % 8
+        prepare_up(other)
+        up_copy(other).start()
         return carry
 
     lax.fori_loop(1, 8, up_start, 0)
+    prepare_up(tile)
     pltpu.make_async_copy(up_ref.at[tile], gbuf.at[pl.ds(1 + 2 * col, 2), :, rows], up_recv.at[tile]).start()
 
     def main_copy(other):
@@ -373,11 +368,35 @@
         return ((tile + shift) % 8) * 4 + (head + place) % 4
 
     def main_start(place, carry):
-        main_copy(main_peer(place)).start()
-        return carry
-
-    lax.fori_loop(0, 28, main_start, 0)
+        other = main_peer(place)
+        prepare((other % 4) * 10 + other // 4)
+        main_copy(other).start()
+        return carry
+
+    lax.fori_loop(0, 16, main_start, 0)
+
+    def ext_arrive(frame, carry):
+        landing(qkv.at[:, pl.ds(11, 2), frame], ext_recv.at[frame]).wait()
+        return carry
+
+    lax.fori_loop(0, 8, ext_arrive, 0)
+
+    def side_copy(side):
+        source, target, step = ((12, 10, 1), (11, 13, -1))[side]
+        return push(qkv.at[pl.ds(1, 2), source], qkv.at[pl.ds(1, 2), target],
+                    side_send.at[side], side_recv.at[side], tile + step, head)
+
+    @pl.when(col < 3)
+    def _():
+        side_copy(0).start()
+
+    @pl.when(col > 0)
+    def _():
+        side_copy(1).start()
+
+    lax.fori_loop(16, 28, main_start, 0)
     lax.fori_loop(29, 32, main_start, 0)
+    prepare(head * 10 + tile)
     pltpu.make_async_copy(send_ref.at[head * 10 + tile], qkv.at[:, pl.ds(1 + 2 * head, 2), tile],
                           main_recv.at[me]).start()
 
@@ -452,29 +471,36 @@
             def _(other=other):
                 out_copy(pair, other).start()
 
-    def outx_copy(half):
-        return push(obuf.at[:, pl.ds(11, 2), :, pl.ds(16 * half, 16)], landed.at[:, 8 + row_half],
-                    outx_send.at[half], outx_recv.at[row_half], 4 * half + col, head)
-
-    def rim_copy(half, side):
+    def outx_piece(pair, half):
+        return obuf.at[pl.ds(2 * pair, 2), pl.ds(11, 2), :, pl.ds(16 * half, 16)]
+
+    def outx_copy(pair, half):
+        return push(outx_piece(pair, half), landed.at[pl.ds(2 * pair, 2), 8 + row_half],
+                    outx_send.at[pair, half], outx_recv.at[pair, row_half], 4 * half + col, head)
+
+    def outx_start(pair):
+        for half in range(2):
+            @pl.when(row_half == half)
+            def _(half=half):
+                pltpu.make_async_copy(outx_piece(pair, half), landed.at[pl.ds(2 * pair, 2), 8 + row_half],
+                                      outx_recv.at[pair, row_half]).start()
+
+            @pl.when(row_half != half)
+            def _(half=half):
+                outx_copy(pair, half).start()
+
+    def rim_copy(side):
         slot, step = ((13, 1), (10, -1))[side]
-        return push(obuf.at[pl.ds(2, 2), slot, :, pl.ds(16 * half, 16)], rims.at[row_half, side],
-                    rim_send.at[half, side], rim_recv.at[row_half, side], 4 * half + col + step, head)
-
-    def ext_arrive(frame, carry):
-        landing(qkv.at[:, pl.ds(11, 2), frame], ext_recv.at[frame]).wait()
-
-        @pl.when(col > 0)
-        def _():
-            landing(qkv.at[pl.ds(1, 2), 10, frame], left_recv.at[frame]).wait()
-
-        @pl.when(col < 3)
-        def _():
-            landing(qkv.at[pl.ds(1, 2), 13, frame], right_recv.at[frame]).wait()
-
-        return carry
-
-    lax.fori_loop(0, 8, ext_arrive, 0)
+        return push(obuf.at[pl.ds(2, 2), slot], rims.at[side], rim_send.at[side], rim_recv.at[side],
+                    tile + step, head)
+
+    @pl.when(col > 0)
+    def _():
+        landing(qkv.at[pl.ds(1, 2), 10], side_recv.at[0]).wait()
+
+    @pl.when(col < 3)
+    def _():
+        landing(qkv.at[pl.ds(1, 2), 13], side_recv.at[1]).wait()
 
     for half in range(2):
         landing(gbuf.at[pl.ds(11, 2), :, pl.ds(16 * half, 16)], upx_recv.at[half]).wait()
@@ -484,34 +510,35 @@
         return carry
 
     lax.fori_loop(8, 10, ext_tile, 0)
-    for slot in range(10, SLOTS):
-        settle(slot)
-    for half in range(2):
-        @pl.when(row_half == half)
-        def _(half=half):
-            pltpu.make_async_copy(obuf.at[:, pl.ds(11, 2), :, pl.ds(16 * half, 16)], landed.at[:, 8 + row_half],
-                                  outx_recv.at[row_half]).start()
-
-        @pl.when(row_half != half)
-        def _(half=half):
-            outx_copy(half).start()
+    settle(10)
+    settle(13)
+
+    @pl.when(col < 3)
+    def _():
+        rim_copy(0).start()
+
+    @pl.when(col > 0)
+    def _():
+        rim_copy(1).start()
+
+    outx_start(0)
+
+    def finish_shared():
+        @pl.when(col > 0)
+        def _():
+            landing(rims.at[0], rim_recv.at[0]).wait()
+            for part in range(2):
+                acc[part, 11] += rims[0, part].reshape(256, HEAD_DIM).astype(jnp.float32)
 
         @pl.when(col < 3)
-        def _(half=half):
-            rim_copy(half, 0).start()
-
-        @pl.when(col > 0)
-        def _(half=half):
-            rim_copy(half, 1).start()
-
-    for extra in range(2):
-        @pl.when(col == 0)
-        def _(extra=extra):
-            rims[extra, 0] = jnp.zeros((2, FRAMES, 16, HEAD_DIM), jnp.bfloat16)
-
-        @pl.when(col == 3)
-        def _(extra=extra):
-            rims[extra, 1] = jnp.zeros((2, FRAMES, 16, HEAD_DIM), jnp.bfloat16)
+        def _():
+            landing(rims.at[1], rim_recv.at[1]).wait()
+            for part in range(2):
+                acc[part, 12] += rims[1, part].reshape(256, HEAD_DIM).astype(jnp.float32)
+
+        settle(11)
+        settle(12)
+        outx_start(1)
 
     def main_arrive(other, carry):
         landing(qkv.at[:, pl.ds(1 + 2 * (other % 4), 2), other // 4], main_recv.at[other]).wait()
@@ -540,43 +567,24 @@
         def _():
             settle_column((col + step // 2 - 1) % 4)
 
+        @pl.when(step == 3)
+        def _():
+            finish_shared()
+
         return carry
 
     lax.fori_loop(0, 8, main_tile, 0)
     settle_column((col + 3) % 4)
     settle_column(col)
 
-    upper = lax.broadcasted_iota(jnp.int32, (16, 8, HEAD_DIM), 1) < 4
-
     def place(ref, which, near, far):
-        near = near.reshape(16, 8, HEAD_DIM)
-        far = far.reshape(16, 8, HEAD_DIM)
-        even = jnp.where(upper, near, pltpu.roll(far, 4, 1))
-        odd = jnp.where(upper, pltpu.roll(near, 4, 1), far)
-        lines = jnp.stack((even, odd), axis=1).reshape(256, HEAD_DIM)
-        ref[:, pl.ds(pl.multiple_of(which * HEAD_DIM, HEAD_DIM), HEAD_DIM)] = lines.astype(jnp.bfloat16)
+        even, odd = regroup(near.reshape(16, 8, HEAD_DIM), far.reshape(16, 8, HEAD_DIM))
+        ref[:, lanes(which)] = jnp.stack((even, odd), axis=1).reshape(256, HEAD_DIM).astype(jnp.bfloat16)
 
     out_refs = (attended_ref, query_ref, key_ref, value_ref)
 
     def wide(part, which, side):
         return landed[part, which, side].astype(jnp.float32)
-
-    for extra in range(2):
-        landing(landed.at[:, 8 + extra], outx_recv.at[extra]).wait()
-
-        @pl.when(col > 0)
-        def _(extra=extra):
-            landing(rims.at[extra, 0], rim_recv.at[extra, 0]).wait()
-
-        @pl.when(col < 3)
-        def _(extra=extra):
-            landing(rims.at[extra, 1], rim_recv.at[extra, 1]).wait()
-
-        for part in range(2):
-            place(out_refs[part], 8 + extra, wide(part, 8 + extra, 0), wide(part, 8 + extra, 1))
-            place(out_refs[2 + part], 8 + extra,
-                  wide(2 + part, 8 + extra, 0) + rims[extra, 0, part].astype(jnp.float32),
-                  wide(2 + part, 8 + extra, 1) + rims[extra, 1, part].astype(jnp.float32))
 
     for pair in range(2):
         def out_arrive(step, carry, pair=pair):
@@ -587,6 +595,10 @@
             return carry
 
         lax.fori_loop(0, 8, out_arrive, 0)
+        for extra in range(2):
+            landing(landed.at[pl.ds(2 * pair, 2), 8 + extra], outx_recv.at[pair, extra]).wait()
+            for part in (2 * pair, 2 * pair + 1):
+                place(out_refs[part], 8 + extra, wide(part, 8 + extra, 0), wide(part, 8 + extra, 1))
 
     def main_left(step, carry):
         main_copy((me + step) % 32).wait_send()
@@ -606,14 +618,6 @@
         @pl.when(jnp.logical_not(ext_is_own(which)))
         def _():
             ext_copy(which).wait_send()
-
-        @pl.when((head < 3) & jnp.logical_not(left_is_own(which)))
-        def _():
-            left_copy(which).wait_send()
-
-        @pl.when((head > 0) & jnp.logical_not(right_is_own(which)))
-        def _():
-            right_copy(which).wait_send()
 
         return carry
 
@@ -622,47 +626,45 @@
         @pl.when(row_half != half)
         def _(half=half):
             upx_copy(half).wait_send()
-            outx_copy(half).wait_send()
-
-        @pl.when(col < 3)
-        def _(half=half):
-            rim_copy(half, 0).wait_send()
-
-        @pl.when(col > 0)
-        def _(half=half):
-            rim_copy(half, 1).wait_send()
+            outx_copy(0, half).wait_send()
+            outx_copy(1, half).wait_send()
+
+    @pl.when(col < 3)
+    def _():
+        side_copy(0).wait_send()
+        rim_copy(0).wait_send()
+
+    @pl.when(col > 0)
+    def _():
+        side_copy(1).wait_send()
+        rim_copy(1).wait_send()
 
 
 def fast_local(query_slab, key_slab, value_slab, upstream):
-    def by_head(slab):
-        shaped = slab.reshape(4, 2, 2, 4, 40, HEAD_DIM).transpose(4, 2, 1, 0, 3, 5)
-        return shaped.reshape(40, 2, 32, HEAD_DIM)
-
-    send = jnp.stack((by_head(query_slab), by_head(key_slab), by_head(value_slab)), axis=1)
-    up = upstream.reshape(FRAMES, 4, 2, 4, 10, HEAD_DIM).transpose(4, 2, 0, 1, 3, 5)
-    up = up.reshape(10, 2, FRAMES, 16, HEAD_DIM)
     dma = pltpu.SemaphoreType.DMA
     out = pl.pallas_call(
         fast_kernel,
         out_shape=[jax.ShapeDtypeStruct((256, 10 * HEAD_DIM), jnp.bfloat16)] * 4,
-        in_specs=[pl.BlockSpec(memory_space=pltpu.VMEM)] * 2,
+        in_specs=[pl.BlockSpec(memory_space=pltpu.VMEM)] * 4,
         out_specs=[pl.BlockSpec(memory_space=pltpu.VMEM)] * 4,
         scratch_shapes=[
+            pltpu.VMEM((40, 3, 2, 32, HEAD_DIM), jnp.bfloat16),
+            pltpu.VMEM((10, 2, FRAMES, 16, HEAD_DIM), jnp.bfloat16),
             pltpu.VMEM((3, SLOTS, FRAMES, 32, HEAD_DIM), jnp.bfloat16),
             pltpu.VMEM((SLOTS, FRAMES, 32, HEAD_DIM), jnp.bfloat16),
             pltpu.VMEM((4, SLOTS, FRAMES, 32, HEAD_DIM), jnp.bfloat16),
             pltpu.VMEM((2, SLOTS, 256, HEAD_DIM), jnp.float32),
             pltpu.VMEM((4, 10, 2, FRAMES, 16, HEAD_DIM), jnp.bfloat16),
-            pltpu.VMEM((2, 2, 2, FRAMES, 16, HEAD_DIM), jnp.bfloat16),
-            dma((32,)), dma((32,)), dma((8,)), dma((8,)), dma((8,)), dma((8,)), dma((8,)), dma((8,)),
-            dma((8,)), dma((8,)), dma((2,)), dma((2,)), dma((2, 8)), dma((2, 8)), dma((2,)), dma((2,)),
-            dma((2, 2)), dma((2, 2)),
+            pltpu.VMEM((2, 2, FRAMES, 32, HEAD_DIM), jnp.bfloat16),
+            dma((32,)), dma((32,)), dma((8,)), dma((8,)), dma((2,)), dma((2,)),
+            dma((8,)), dma((8,)), dma((2,)), dma((2,)), dma((2, 8)), dma((2, 8)), dma((2, 2)), dma((2, 2)),
+            dma((2,)), dma((2,)),
         ],
         compiler_params=pltpu.CompilerParams(
             collective_id=0, has_side_effects=True, vmem_limit_bytes=48 * 1024 * 1024
         ),
         cost_estimate=pl.CostEstimate(flops=3 * 10**9, bytes_accessed=8 * 10**6, transcendentals=2 * 10**6),
-    )(send, up)
+    )(query_slab, key_slab, value_slab, upstream)
     return tuple(out)
 
 

time: 141 us -> 132 us (0.936)
  Pallas kernels: 132 us -> 123 us
    pallas_call x1, Pallas kernels: 132 us -> 123 us  [fast_local(): pl.pallas_call(fast_kernel, out_shape=[jax.ShapeDtypeStruct((256, 10 * HE...]
    unnamed x11 -> x12, local copies, waits for them, and re-layouts: 5.05 us -> 7.69 us
    reshape x4 -> x0, local copies, waits for them, and re-layouts: 2.5 us -> none  [the longest x1 1.46 us: fast_local(): upstream.reshape(FRAMES, 4, 2, 4, 10, HEAD_DIM).transpose(4, 2, 0, 1, 3, 5)]
where the time goes in v3:
time: 132 us
  Pallas kernels  123 us (93%)
  local copies, waits for them, and re-layouts  7.69 us (6%)
    pallas_call x1, Pallas kernels, fast_local(): pl.pallas_call(fast_kernel, out_shape=[jax.ShapeDtypeStruct((256, 10 * HE...  123 us
    unnamed x12, local copies, waits for them, and re-layouts  7.69 us

profile of v3, /device:TPU:0, one launch (start us, length us, event | category | flops | bytes accessed | tf_op | source)
XLA Modules:
  0.0 131.7 jit_solution(11820642864885316440)
XLA Ops:
  0.6 0.0 copy-start
  0.6 1.1 copy-done
  1.7 0.0 copy-start.1
  1.7 1.1 copy-done.1
  2.8 0.0 copy-start.2
  2.8 1.1 copy-done.2
  3.9 0.0 copy-start.3
  3.9 1.1 copy-done.3
  5.0 123.4 %shard_map.75 = (bf16[256,1280]{1,0:T(8,128)(2,1)S(1)}, bf16[256,1280]{1,0:T(8,128)(2,1)S(1)}, bf16[256,1280]{1,0:T(8,128)(2,1)S(1)}, bf16[256,1280]{1,0:T(8,128)(2,1)S(1)}) custom-call(bf16[4,2,8,5120]{3,2,1,0:T(8,128)(2,1)S(1)} %copy-done, bf16[4,2,8,5120]{3,2,1,0:T(8,128)(2,1)S(1)} %copy-done.1, bf16[4,2,8,5120]{3,2,1,0:T(8,128)(2,1)S(1)} %copy-done.2, ...), custom_call_target="tpu_custom_call" | custom-call | flops 3000000000 | bytes 8000000 | tf_op jit(solution)/shard_map/pallas_call | solution.py:645
  128.4 0.8 copy.12
  129.2 0.8 copy.13
  130.0 0.8 copy.14
  130.9 0.8 copy.15
Async XLA Ops:
  0.6 1.1 copy-start
  1.7 1.1 copy-start.1
  2.8 1.1 copy-start.2
  3.9 1.1 copy-start.3

commit v4 on v3

--- a/solution.py
+++ b/solution.py
@@ -238,17 +238,33 @@
 SLOTS = 14
 
 
-def fast_kernel(query_slab, key_slab, value_slab, grad_in, attended_ref, query_ref, key_ref, value_ref,
-                send_ref, up_ref, qkv, gbuf, obuf, acc, landed, rims,
+def fast_kernel(query_hbm, key_hbm, value_hbm, grad_hbm, attended_ref, query_ref, key_ref, value_ref,
+                slabs, grad_in, results, send_ref, up_ref, qkv, gbuf, obuf, acc, landed, rims,
                 main_send, main_recv, ext_send, ext_recv, side_send, side_recv,
                 up_send, up_recv, upx_send, upx_recv, out_send, out_recv, outx_send, outx_recv,
-                rim_send, rim_recv):
+                rim_send, rim_recv, slab_sem, grad_sem, done_sem):
     tile = lax.axis_index("tile")
     head = lax.axis_index("head")
     me = tile * 4 + head
     row_half = tile // 4
     col = tile % 4
 
+    def slab_copy(part, group):
+        lanes_of = pl.ds(group * 10 * HEAD_DIM, 10 * HEAD_DIM)
+        source = (query_hbm, key_hbm, value_hbm)[part]
+        return pltpu.make_async_copy(source.at[:, :, :, lanes_of], slabs.at[part, :, :, :, lanes_of],
+                                     slab_sem.at[part, group])
+
+    def grad_copy(quarter):
+        rows_of = pl.ds(64 * quarter, 64)
+        return pltpu.make_async_copy(grad_hbm.at[rows_of], grad_in.at[rows_of], grad_sem.at[quarter])
+
+    for group in range(4):
+        for part in range(3):
+            slab_copy(part, group).start()
+    for quarter in range(4):
+        grad_copy(quarter).start()
+
     barrier = pltpu.get_barrier_semaphore()
 
     def greet(step, carry):
@@ -268,8 +284,8 @@
         return pl.ds(pl.multiple_of(which * HEAD_DIM, HEAD_DIM), HEAD_DIM)
 
     def prepare(which):
-        for part, slab in enumerate((query_slab, key_slab, value_slab)):
-            lines = slab[:, :, :, lanes(which)].astype(jnp.float32).reshape(2, 2, 16, HEAD_DIM)
+        for part in range(3):
+            lines = slabs[part, :, :, :, lanes(which)].astype(jnp.float32).reshape(2, 2, 16, HEAD_DIM)
             first = lines[:, 0].reshape(4, 8, HEAD_DIM)
             second = lines[:, 1].reshape(4, 8, HEAD_DIM)
             for side, taken in enumerate(regroup(first, second)):
@@ -285,6 +301,9 @@
         prepare((which // 2) * 10 + 8 + which % 2)
         return carry
 
+    for group in range(4):
+        for part in range(3):
+            slab_copy(part, group).wait()
     lax.fori_loop(0, 8, prepare_shared, 0)
     pl.semaphore_wait(barrier, 31)
 
@@ -330,6 +349,8 @@
         return push(up_ref.at[8 + extra], gbuf.at[pl.ds(11, 2), :, rows],
                     upx_send.at[extra], upx_recv.at[row_half], 4 * extra + col, head)
 
+    for quarter in range(4):
+        grad_copy(quarter).wait()
     for extra in range(2):
         prepare_up(8 + extra)
 
@@ -363,14 +384,24 @@
         return push(src, dst, main_send.at[other], main_recv.at[me], to_tile, to_head)
 
     def main_peer(place):
-        turn = place // 4
-        shift = 12 + ((turn + 1) // 2) * (2 * (turn % 2) - 1)
-        return ((tile + shift) % 8) * 4 + (head + place) % 4
+        turn = place // 8
+        column = (head + turn + turn // 2 - 2 * (turn // 3)) % 4
+        other_tile = 4 * ((row_half + 1 - (place % 8) // 4) % 2) + column
+        return other_tile * 4 + (head + place) % 4
 
     def main_start(place, carry):
         other = main_peer(place)
         prepare((other % 4) * 10 + other // 4)
-        main_copy(other).start()
+
+        @pl.when(other != me)
+        def _():
+            main_copy(other).start()
+
+        @pl.when(other == me)
+        def _():
+            pltpu.make_async_copy(send_ref.at[head * 10 + tile], qkv.at[:, pl.ds(1 + 2 * head, 2), tile],
+                                  main_recv.at[me]).start()
+
         return carry
 
     lax.fori_loop(0, 16, main_start, 0)
@@ -394,11 +425,7 @@
     def _():
         side_copy(1).start()
 
-    lax.fori_loop(16, 28, main_start, 0)
-    lax.fori_loop(29, 32, main_start, 0)
-    prepare(head * 10 + tile)
-    pltpu.make_async_copy(send_ref.at[head * 10 + tile], qkv.at[:, pl.ds(1 + 2 * head, 2), tile],
-                          main_recv.at[me]).start()
+    lax.fori_loop(16, 32, main_start, 0)
 
     blank = jnp.zeros((FRAMES, 32, HEAD_DIM), jnp.bfloat16)
     for part in (1, 2):
@@ -540,11 +567,13 @@
         settle(12)
         outx_start(1)
 
-    def main_arrive(other, carry):
-        landing(qkv.at[:, pl.ds(1 + 2 * (other % 4), 2), other // 4], main_recv.at[other]).wait()
-        return carry
-
-    lax.fori_loop(0, 32, main_arrive, 0)
+    def main_arrive(place, carry):
+        column = (col + 3 + place // 8) % 4
+        frame = place % 8
+        landing(qkv.at[:, pl.ds(1 + 2 * column, 2), frame], main_recv.at[frame * 4 + column]).wait()
+        return carry
+
+    lax.fori_loop(0, 24, main_arrive, 0)
 
     def up_arrive(other, carry):
         landing(gbuf.at[pl.ds(1 + 2 * (other % 4), 2), :, pl.ds(16 * (other // 4), 16)], up_recv.at[other]).wait()
@@ -557,6 +586,10 @@
         out_start(1, column)
 
     def main_tile(step, carry):
+        @pl.when(step == 3)
+        def _():
+            lax.fori_loop(24, 32, main_arrive, 0)
+
         one_tile((step + 2 * col) % 8)
 
         @pl.when(step % 2 == 1)
@@ -577,11 +610,17 @@
     settle_column((col + 3) % 4)
     settle_column(col)
 
-    def place(ref, which, near, far):
+    out_refs = (attended_ref, query_ref, key_ref, value_ref)
+
+    def result_copy(part, which):
+        return pltpu.make_async_copy(results.at[part, :, lanes(which)], out_refs[part].at[:, lanes(which)],
+                                     done_sem.at[part, which])
+
+    def place(part, which, near, far):
         even, odd = regroup(near.reshape(16, 8, HEAD_DIM), far.reshape(16, 8, HEAD_DIM))
-        ref[:, lanes(which)] = jnp.stack((even, odd), axis=1).reshape(256, HEAD_DIM).astype(jnp.bfloat16)
-
-    out_refs = (attended_ref, query_ref, key_ref, value_ref)
+        lines = jnp.stack((even, odd), axis=1).reshape(256, HEAD_DIM)
+        results[part, :, lanes(which)] = lines.astype(jnp.bfloat16)
+        result_copy(part, which).start()
 
     def wide(part, which, side):
         return landed[part, which, side].astype(jnp.float32)
@@ -591,14 +630,21 @@
             other = (tile + step) % 8
             landing(landed.at[pl.ds(2 * pair, 2), other], out_recv.at[pair, other]).wait()
             for part in (2 * pair, 2 * pair + 1):
-                place(out_refs[part], other, wide(part, other, 0), wide(part, other, 1))
+                place(part, other, wide(part, other, 0), wide(part, other, 1))
             return carry
 
         lax.fori_loop(0, 8, out_arrive, 0)
         for extra in range(2):
             landing(landed.at[pl.ds(2 * pair, 2), 8 + extra], outx_recv.at[pair, extra]).wait()
             for part in (2 * pair, 2 * pair + 1):
-                place(out_refs[part], 8 + extra, wide(part, 8 + extra, 0), wide(part, 8 + extra, 1))
+                place(part, 8 + extra, wide(part, 8 + extra, 0), wide(part, 8 + extra, 1))
+
+    def results_done(which, carry):
+        for part in range(4):
+            result_copy(part, which).wait()
+        return carry
+
+    lax.fori_loop(0, 10, results_done, 0)
 
     def main_left(step, carry):
         main_copy((me + step) % 32).wait_send()
@@ -640,14 +686,32 @@
         rim_copy(1).wait_send()
 
 
+def write_kernel(*refs):
+    sources, targets, sems = refs[:4], refs[4:8], refs[8]
+    copies = [
+        pltpu.make_async_copy(
+            sources[part].at[pl.ds(64 * quarter, 64)], targets[part].at[pl.ds(64 * quarter, 64)], sems.at[part, quarter]
+        )
+        for quarter in range(4)
+        for part in range(4)
+    ]
+    for copy in copies:
+        copy.start()
+    for copy in copies:
+        copy.wait()
+
+
 def fast_local(query_slab, key_slab, value_slab, upstream):
     dma = pltpu.SemaphoreType.DMA
     out = pl.pallas_call(
         fast_kernel,
         out_shape=[jax.ShapeDtypeStruct((256, 10 * HEAD_DIM), jnp.bfloat16)] * 4,
-        in_specs=[pl.BlockSpec(memory_space=pltpu.VMEM)] * 4,
-        out_specs=[pl.BlockSpec(memory_space=pltpu.VMEM)] * 4,
+        in_specs=[pl.BlockSpec(memory_space=pltpu.HBM)] * 4,
+        out_specs=[pl.BlockSpec(memory_space=pltpu.HBM)] * 4,
         scratch_shapes=[
+            pltpu.VMEM((3, 4, 2, 8, 40 * HEAD_DIM), jnp.bfloat16),
+            pltpu.VMEM((256, 10 * HEAD_DIM), jnp.bfloat16),
+            pltpu.VMEM((4, 256, 10 * HEAD_DIM), jnp.bfloat16),
             pltpu.VMEM((40, 3, 2, 32, HEAD_DIM), jnp.bfloat16),
             pltpu.VMEM((10, 2, FRAMES, 16, HEAD_DIM), jnp.bfloat16),
             pltpu.VMEM((3, SLOTS, FRAMES, 32, HEAD_DIM), jnp.bfloat16),
@@ -658,14 +722,24 @@
             pltpu.VMEM((2, 2, FRAMES, 32, HEAD_DIM), jnp.bfloat16),
             dma((32,)), dma((32,)), dma((8,)), dma((8,)), dma((2,)), dma((2,)),
             dma((8,)), dma((8,)), dma((2,)), dma((2,)), dma((2, 8)), dma((2, 8)), dma((2, 2)), dma((2, 2)),
-            dma((2,)), dma((2,)),
+            dma((2,)), dma((2,)), dma((3, 4)), dma((4,)), dma((4, 10)),
         ],
         compiler_params=pltpu.CompilerParams(
-            collective_id=0, has_side_effects=True, vmem_limit_bytes=48 * 1024 * 1024
+            collective_id=0, has_side_effects=True, vmem_limit_bytes=61 * 1024 * 1024
         ),
         cost_estimate=pl.CostEstimate(flops=3 * 10**9, bytes_accessed=8 * 10**6, transcendentals=2 * 10**6),
     )(query_slab, key_slab, value_slab, upstream)
-    return tuple(out)
+    return tuple(
+        pl.pallas_call(
+            write_kernel,
+            out_shape=[jax.ShapeDtypeStruct((256, 10 * HEAD_DIM), jnp.bfloat16)] * 4,
+            in_specs=[pl.BlockSpec(memory_space=pltpu.HBM)] * 4,
+            out_specs=[pl.BlockSpec(memory_space=pltpu.HBM)] * 4,
+            scratch_shapes=[dma((4, 4))],
+            compiler_params=pltpu.CompilerParams(vmem_limit_bytes=61 * 1024 * 1024),
+            cost_estimate=pl.CostEstimate(flops=0, bytes_accessed=5 * 10**6, transcendentals=0),
+        )(*out)
+    )
 
 
 def solution(mesh):

time: 132 us -> 206 us (1.56)
  Pallas kernels: 123 us -> 205 us
  local copies, waits for them, and re-layouts: 7.69 us -> 0 us
    pallas_call x0 -> x1, Pallas kernels: none -> 80.7 us  [fast_local(): pl.pallas_call(write_kernel, out_shape=[jax.ShapeDtypeStruct((256, 10 * H...]
    unnamed x12 -> x0, local copies, waits for them, and re-layouts: 7.69 us -> none
where the time goes in v4:
time: 206 us
  Pallas kernels  205 us (100%)
    pallas_call x1, Pallas kernels, fast_local(): pl.pallas_call(fast_kernel, out_shape=[jax.ShapeDtypeStruct((256, 10 * HE...  125 us
    pallas_call x1, Pallas kernels, fast_local(): pl.pallas_call(write_kernel, out_shape=[jax.ShapeDtypeStruct((256, 10 * H...  80.7 us

profile of v4, /device:TPU:0, one launch (start us, length us, event | category | flops | bytes accessed | tf_op | source)
XLA Modules:
  0.0 206.1 jit_solution(8990880920679497845)
XLA Ops:
  0.6 124.8 %shard_map.75 = (bf16[256,1280]{1,0:T(8,128)(2,1)}, bf16[256,1280]{1,0:T(8,128)(2,1)}, bf16[256,1280]{1,0:T(8,128)(2,1)}, bf16[256,1280]{1,0:T(8,128)(2,1)}) custom-call(bf16[4,2,8,5120]{3,2,1,0:T(8,128)(2,1)} %query_hbm.1, bf16[4,2,8,5120]{3,2,1,0:T(8,128)(2,1)} %key_hbm.1, bf16[4,2,8,5120]{3,2,1,0:T(8,128)(2,1)} %value_hbm.1, bf16[256,1280]{1,0:T(8,128)(2,1)} %grad_hbm.1), custom_call_target="tpu_custom_call" | custom-call | flops 3000000000 | bytes 8000000 | tf_op jit(solution)/shard_map/pallas_call | solution.py:706
  125.5 80.7 %shard_map.76 = (bf16[256,1280]{1,0:T(8,128)(2,1)}, bf16[256,1280]{1,0:T(8,128)(2,1)}, bf16[256,1280]{1,0:T(8,128)(2,1)}, bf16[256,1280]{1,0:T(8,128)(2,1)}) custom-call(bf16[256,1280]{1,0:T(8,128)(2,1)} %get-tuple-element.8.refs_0_, bf16[256,1280]{1,0:T(8,128)(2,1)} %get-tuple-element.9.refs_1_, bf16[256,1280]{1,0:T(8,128)(2,1)} %get-tuple-element.10.refs_2_, ...), custom_call_target="tpu_custom_call" | custom-call | bytes 5000000 | tf_op jit(solution)/shard_map/pallas_call | solution.py:733

commit v5 on v4

--- a/solution.py
+++ b/solution.py
@@ -686,21 +686,6 @@
         rim_copy(1).wait_send()
 
 
-def write_kernel(*refs):
-    sources, targets, sems = refs[:4], refs[4:8], refs[8]
-    copies = [
-        pltpu.make_async_copy(
-            sources[part].at[pl.ds(64 * quarter, 64)], targets[part].at[pl.ds(64 * quarter, 64)], sems.at[part, quarter]
-        )
-        for quarter in range(4)
-        for part in range(4)
-    ]
-    for copy in copies:
-        copy.start()
-    for copy in copies:
-        copy.wait()
-
-
 def fast_local(query_slab, key_slab, value_slab, upstream):
     dma = pltpu.SemaphoreType.DMA
     out = pl.pallas_call(
@@ -729,17 +714,7 @@
         ),
         cost_estimate=pl.CostEstimate(flops=3 * 10**9, bytes_accessed=8 * 10**6, transcendentals=2 * 10**6),
     )(query_slab, key_slab, value_slab, upstream)
-    return tuple(
-        pl.pallas_call(
-            write_kernel,
-            out_shape=[jax.ShapeDtypeStruct((256, 10 * HEAD_DIM), jnp.bfloat16)] * 4,
-            in_specs=[pl.BlockSpec(memory_space=pltpu.HBM)] * 4,
-            out_specs=[pl.BlockSpec(memory_space=pltpu.HBM)] * 4,
-            scratch_shapes=[dma((4, 4))],
-            compiler_params=pltpu.CompilerParams(vmem_limit_bytes=61 * 1024 * 1024),
-            cost_estimate=pl.CostEstimate(flops=0, bytes_accessed=5 * 10**6, transcendentals=0),
-        )(*out)
-    )
+    return tuple(out)
 
 
 def solution(mesh):

time: 206 us -> 131 us (0.64)
  Pallas kernels: 205 us -> 125 us
  local copies, waits for them, and re-layouts: 0 us -> 5.52 us
    pallas_call x1 -> x0, Pallas kernels: 80.7 us -> none  [fast_local(): pl.pallas_call(write_kernel, out_shape=[jax.ShapeDtypeStruct((256, 10 * H...]
    unnamed x0 -> x10, local copies, waits for them, and re-layouts: none -> 5.52 us
where the time goes in v5:
time: 131 us
  Pallas kernels  125 us (95%)
  local copies, waits for them, and re-layouts  5.52 us (4%)
    pallas_call x1, Pallas kernels, fast_local(): pl.pallas_call(fast_kernel, out_shape=[jax.ShapeDtypeStruct((256, 10 * HE...  125 us
    unnamed x10, local copies, waits for them, and re-layouts  5.52 us

profile of v5, /device:TPU:0, one launch (start us, length us, event | category | flops | bytes accessed | tf_op | source)
XLA Modules:
  0.0 131.0 jit_solution(13135548520730851503)
XLA Ops:
  0.6 124.8 %shard_map.75 = (bf16[256,1280]{1,0:T(8,128)(2,1)}, bf16[256,1280]{1,0:T(8,128)(2,1)}, bf16[256,1280]{1,0:T(8,128)(2,1)}, bf16[256,1280]{1,0:T(8,128)(2,1)}) custom-call(bf16[4,2,8,5120]{3,2,1,0:T(8,128)(2,1)} %query_hbm.1, bf16[4,2,8,5120]{3,2,1,0:T(8,128)(2,1)} %key_hbm.1, bf16[4,2,8,5120]{3,2,1,0:T(8,128)(2,1)} %value_hbm.1, bf16[256,1280]{1,0:T(8,128)(2,1)} %grad_hbm.1), custom_call_target="tpu_custom_call" | custom-call | flops 3000000000 | bytes 8000000 | tf_op jit(solution)/shard_map/pallas_call | solution.py:691
  125.4 0.0 copy-start.2
  125.5 2.0 %copy.12 = bf16[256,1280]{1,0:T(8,128)(2,1)} copy(bf16[256,1280]{1,0:T(8,128)(2,1)} %get-tuple-element.8) | data formatting | bytes 1310720
  127.5 0.0 copy-done.2
  127.5 0.0 copy-start.1
  127.5 0.8 copy.13
  128.3 0.5 copy-done.1
  128.8 0.0 copy-start
  128.8 0.8 copy.14
  129.7 0.5 copy-done
  130.1 0.8 copy.15
Async XLA Ops:
  125.4 2.0 %copy-start.2 = (bf16[256,1280]{1,0:T(8,128)(2,1)S(1)}, bf16[256,1280]{1,0:T(8,128)(2,1)}, u32[]{:S(2)}) copy-start(bf16[256,1280]{1,0:T(8,128)(2,1)} %get-tuple-element.9) | copy-start | bytes 1966084
  127.5 1.3 %copy-start.1 = (bf16[256,1280]{1,0:T(8,128)(2,1)S(1)}, bf16[256,1280]{1,0:T(8,128)(2,1)}, u32[]{:S(2)}) copy-start(bf16[256,1280]{1,0:T(8,128)(2,1)} %get-tuple-element.10) | copy-start | bytes 1966084
  128.8 1.3 %copy-start = (bf16[256,1280]{1,0:T(8,128)(2,1)S(1)}, bf16[256,1280]{1,0:T(8,128)(2,1)}, u32[]{:S(2)}) copy-start(bf16[256,1280]{1,0:T(8,128)(2,1)} %get-tuple-element.11) | copy-start | bytes 1966084
